TPU v7x, 1024 devices: a whole 4x8x16 slice. The times are simulated.
1024 devices in a mesh: coarse: 16 (over x, z_hi, core), sub: 64 (over z_lo, y).
Axes of the slice: x: 4, y: 8, z: 16 (z_hi: 2, z_lo: 8; z = z_hi * 8 + z_lo), core: 2. Of those that a mesh axis runs over, the one named last changes fastest.
Arguments:
- face_loads: float32 [16, 64, 6, 64, 128], P('coarse', 'sub'), may hold values from -18 to 18
- schur_blocks: float32 [16, 64, 384, 384], P('coarse', 'sub'), may hold values from -8 to 70, as said below
- coarse_basis: float32 [16, 64, 384, 32], P('coarse', 'sub'), may hold values from -0.75 to 0.75
- drop_masks: int32 [16, 64, 6, 64], P('coarse', 'sub'), may hold values 0 or 1
- coarse_inverse: float32 [64, 512, 512], P('sub', 'coarse'), may hold values from -1 to 3, as said below
Outputs:
- solution: float32 [16, 64, 6, 64, 128], P('coarse', 'sub')
- residual: float32 [16, 64, 6, 64, 128], P('coarse', 'sub')
Inputs may be any that keep to these rules, and one draw needn't show every extreme that they name: `schur_blocks`: each subdomain's block is symmetric positive definite. `coarse_inverse`: each group's matrix is symmetric positive definite.
All inputs are finite; a program needn't handle non-finite values. No bound on the sum of `drop_masks` on one device may be relied on, other than what follows from the above.
Results may differ from a plain program's by a relative error of at most 0.0003.
Values sent between devices are 32-bit elements; how exact they have to be, the bound alone decides.
A program may use at most 32 MiB of HBM per device.

v0:
```python
import jax
import jax.numpy as jnp
from jax import lax
from jax.sharding import PartitionSpec as P

ROW = 8
ITERS = 2


highest = lax.Precision.HIGHEST


def padded(cells, sides, width):
    for axis, dim in sides:
        count = lax.axis_size(axis)
        ends = count - 1
        head = lax.slice_in_dim(cells, 0, width, axis=dim)
        tail = lax.slice_in_dim(cells, cells.shape[dim] - width, cells.shape[dim], axis=dim)
        cells = jnp.concatenate(
            [
                lax.ppermute(tail, axis, [(i, (i + 1) % count) for i in range(ends)]),
                cells,
                lax.ppermute(head, axis, [((i + 1) % count, i) for i in range(ends)]),
            ],
            axis=dim,
        )
    return cells


def shifted(value, axis, by):
    count = lax.axis_size(axis)
    pairs = [(i, i + by) for i in range(count) if 0 <= i + by < count]
    return lax.ppermute(value, axis, pairs)


def matmul(former, latter):
    return jnp.dot(former, latter, precision=highest, preferred_element_type=jnp.float32)


def assemble(values):
    coarse_side = padded(values[0:2], (("coarse", 0),), 1)
    row_side = padded(values[2:4], (("sub", 0),), 1)
    column_side = []
    for source_face, offset in ((5, ROW), (4, -ROW)):
        column_side.append(shifted(values[source_face], "sub", offset))
    incoming = jnp.stack(
        [coarse_side[0], coarse_side[3], row_side[0], row_side[3], column_side[0], column_side[1]]
    )
    return values + incoming


def single_sum(partial_terms):
    return lax.psum(partial_terms, ("coarse", "sub"))


def on_device(face_loads, schur_blocks, coarse_basis, drop_masks, coarse_inverse):
    face_count, dof_count, case_count = face_loads.shape[2:]
    order_size = face_count * dof_count
    coarse_place = lax.axis_index("coarse")
    sub_place = lax.axis_index("sub")
    coarse_total = lax.axis_size("coarse")
    sub_total = lax.axis_size("sub")
    present = jnp.stack(
        [
            coarse_place > 0,
            coarse_place < coarse_total - 1,
            sub_place > 0,
            sub_place < sub_total - 1,
            sub_place >= ROW,
            sub_place < sub_total - ROW,
        ]
    )
    weights = jnp.where(present, 0.5, 1.0).astype(jnp.float32)[:, None, None]
    scaling = (1.0 + drop_masks[0, 0].astype(jnp.float32)).reshape(order_size, 1)
    schur_local = schur_blocks[0, 0]
    basis_local = coarse_basis[0, 0]
    rows_inverse = coarse_inverse[0]
    operator = scaling * schur_local * scaling.reshape(1, order_size)
    factor = jnp.linalg.cholesky(operator + matmul(basis_local, basis_local.T))

    def precondition(vector):
        weighted = (weights * vector).reshape(order_size, case_count)
        restricted = matmul(basis_local.T, weighted)
        coarse_part = matmul(rows_inverse, lax.all_gather(restricted, "coarse", axis=0, tiled=True))
        local_part = jax.scipy.linalg.cho_solve((factor, True), weighted)
        combined = local_part + matmul(basis_local, coarse_part)
        return assemble(weights * combined.reshape(face_count, dof_count, case_count))

    def weighted_sum(former, latter):
        return jnp.sum(weights * former * latter, axis=(0, 1))

    spread = face_loads[0, 0]
    residual = assemble(spread)
    solution = jnp.zeros_like(residual)
    precond = precondition(residual)
    direction = precond
    gamma_now = single_sum(weighted_sum(residual, precond))
    for sweep_index in range(ITERS):
        flat = direction.reshape(order_size, case_count)
        local_image = scaling * matmul(schur_local, scaling * flat)
        mapped = assemble(local_image.reshape(face_count, dof_count, case_count))
        step_size = gamma_now / single_sum(weighted_sum(direction, mapped))
        solution = solution + step_size * direction
        residual, spread = (residual - step_size * mapped, spread)
        if sweep_index + 1 < ITERS:
            precond = precondition(residual)
            gamma_next = single_sum(weighted_sum(residual, precond))
            direction = precond + gamma_next / gamma_now * direction
            gamma_now = gamma_next
    return (solution[None, None], residual[None, None])


def solution(mesh):
    return jax.shard_map(
        on_device,
        mesh=mesh,
        in_specs=(
            P("coarse", "sub", None, None, None),
            P("coarse", "sub", None, None),
            P("coarse", "sub", None, None),
            P("coarse", "sub", None, None),
            P("sub", "coarse", None),
        ),
        out_specs=(P("coarse", "sub", None, None, None), P("coarse", "sub", None, None, None)),
        check_vma=False,
    )
```

profile of v0, /device:TPU:1, one launch (start us, length us, event | category | flops | bytes accessed | tf_op | source)
XLA Modules:
  0.0 726.6 jit_solution(11000554207204416506)
XLA Ops:
  0.6 0.9 slice_bitcast_fusion.27
  1.5 20.5 %collective-permute-start = (f32[1,64,128]{2,1,0:T(8,128)S(1)}, f32[1,64,128]{2,1,0:T(8,128)S(1)}, u32[]{:S(2)}, u32[]{:S(2)}) collective-permute-start(f32[1,64,128]{2,1,0:T(8,128)S(1)} %get-tuple-element.60), channel_id=1, source_target_pairs={{0,64},{64,128},{128,192},{192,256},{256,320},{320,384},{384,448},... | collective-permute-start | bytes 98312 | tf_op jit(solution)/shard_map/ppermute | solution.py:21
  22.0 1.9 collective-permute-start.1
  23.9 3.2 collective-permute-start.2
  27.2 1.3 collective-permute-start.3
  28.5 6.0 collective-permute-start.4
  34.6 1.3 copy.14
  35.9 0.7 convolution_add_fusion
  36.9 11.7 %cholesky.77 = f32[128,128]{1,0:T(8,128)S(1)} custom-call(f32[128,128]{1,0:T(8,128)S(1)} %cholesky.192), custom_call_target="Cholesky" | custom-call | tf_op jit(solution)/shard_map/jit(cholesky)/cholesky | solution.py:79
  48.7 9.8 %custom-call.24 = f32[1,128,128]{1,2,0:T(8,128)S(1)} custom-call(f32[1,128,128]{2,1,0:T(8,128)S(1)} %get-tuple-element.67), custom_call_target="InvertDiagBlocksLowerTriangular" | custom-call | tf_op jit(solution)/shard_map/jit(cholesky)/cholesky | solution.py:79
  59.1 11.7 %cholesky.162 = f32[128,128]{1,0:T(8,128)S(1)} custom-call(f32[128,128]{1,0:T(8,128)S(1)} %cholesky.196), custom_call_target="Cholesky" | custom-call | tf_op jit(solution)/shard_map/jit(cholesky)/cholesky | solution.py:79
  70.8 9.9 %custom-call.25 = f32[1,128,128]{1,2,0:T(8,128)S(1)} custom-call(f32[1,128,128]{2,1,0:T(8,128)S(1)} %get-tuple-element.64), custom_call_target="InvertDiagBlocksLowerTriangular" | custom-call | tf_op jit(solution)/shard_map/jit(cholesky)/cholesky | solution.py:79
  81.3 11.7 %cholesky.181 = f32[128,128]{1,0:T(8,128)S(1)} custom-call(f32[128,128]{1,0:T(8,128)S(1)} %convolution_subtract_fusion.9), custom_call_target="Cholesky" | custom-call | tf_op jit(solution)/shard_map/jit(cholesky)/cholesky | solution.py:79
  93.0 0.6 compare_reduce_fusion
  93.7 0.7 compare_reduce_fusion.1
  96.3 5.7 while.4
  96.4 0.5 fusion.93
  96.9 1.3 bitcast_dynamic-update-slice_fusion.2
  98.9 1.3 bitcast_dynamic-update-slice_fusion.2
  100.8 1.3 bitcast_dynamic-update-slice_fusion.2
  102.2 29.5 %custom-call.27 = f32[3,128,128]{1,2,0:T(8,128)S(1)} custom-call(f32[3,128,128]{2,1,0:T(8,128)S(1)} %get-tuple-element.17), custom_call_target="InvertDiagBlocksLowerTriangular" | custom-call | tf_op jit(solution)/shard_map/jit(_cho_solve)/triangular_solve | solution.py:85
  131.9 1.4 collective-permute-start.5
  133.4 3.3 collective-permute-done.5
  139.8 51.5 %all_gather.6 = f32[512,128]{1,0:T(8,128)S(1)} all-gather(f32[32,128]{1,0:T(8,128)S(1)} %convolution_bitcast_fusion.3), channel_id=1, replica_groups=mesh['coarse'=16,'sub'=64] {'coarse'}, dimensions={0}, use_global_device_ids=true | all-gather | bytes 278528 | tf_op jit(solution)/shard_map/all_gather | solution.py:84
  191.3 0.6 fusion.41
  192.5 1.9 collective-permute-start.6
  194.4 2.4 collective-permute-start.7
  196.8 1.3 collective-permute-start.8
  198.1 1.3 collective-permute-start.9
  199.4 5.7 collective-permute-start.10
  205.2 1.6 collective-permute-start.11
  206.9 1.5 collective-permute-done.7
  208.4 4.6 collective-permute-done.11
  213.2 0.7 convolution_multiply_fusion.1
  213.9 13.6 %collective-permute-start.12 = (f32[1,64,128]{2,1,0:T(8,128)S(1)}, f32[1,64,128]{2,1,0:T(8,128)S(1)}, u32[]{:S(2)}, u32[]{:S(2)}) collective-permute-start(f32[1,64,128]{2,1,0:T(8,128)S(1)} %get-tuple-element.48), channel_id=1, source_target_pairs={{0,64},{64,128},{128,192},{192,256},{256,320},{320,384},{384,448},... | collective-permute-start | bytes 98312 | tf_op jit(solution)/shard_map/ppermute | solution.py:21
  227.8 1.9 collective-permute-start.13
  229.7 1.3 collective-permute-start.14
  231.0 1.3 collective-permute-start.15
  232.3 8.4 %collective-permute-start.16 = (f32[64,128]{1,0:T(8,128)S(1)}, f32[64,128]{1,0:T(8,128)S(1)}, u32[]{:S(2)}, u32[]{:S(2)}) collective-permute-start(f32[64,128]{1,0:T(8,128)S(1)} %get-tuple-element.44), channel_id=1, source_target_pairs={{0,8},{1,9},{2,10},{3,11},{4,12},{5,13},{6,14},{7,15},{8,16},{9,17... | collective-permute-start | bytes 98312 | tf_op jit(solution)/shard_map/ppermute | solution.py:33
  240.7 1.3 collective-permute-start.17
  242.1 3.3 collective-permute-done.17
  245.5 130.3 %all-reduce.1 = (f32[128]{0:T(128)S(1)}, f32[128]{0:T(128)S(1)}) all-reduce(f32[128]{0:T(128)S(1)} %multiply_reduce_fusion.2, f32[128]{0:T(128)S(1)} %multiply_reduce_fusion.1), channel_id=1, replica_groups=mesh['coarse'=16,'sub'=64] {'coarse','sub'}, use_global_device_ids=true, to_apply=%region_7.9 | all-reduce | flops 256 | bytes 2048 | tf_op jit(solution)/shard_map/psum | solution.py:53
  378.9 42.0 %all_gather.7 = f32[512,128]{1,0:T(8,128)S(1)} all-gather(f32[32,128]{1,0:T(8,128)S(1)} %convolution_bitcast_fusion.2), channel_id=1, replica_groups=mesh['coarse'=16,'sub'=64] {'coarse'}, dimensions={0}, use_global_device_ids=true | all-gather | bytes 278528 | tf_op jit(solution)/shard_map/all_gather | solution.py:84
  420.8 0.6 fusion.39
  422.0 5.8 collective-permute-start.18
  427.8 1.9 collective-permute-start.19
  429.8 1.3 collective-permute-start.20
  431.1 1.3 collective-permute-start.21
  432.4 7.2 collective-permute-start.22
  439.7 1.3 collective-permute-start.23
  441.0 0.8 collective-permute-done.19
  441.9 2.5 collective-permute-done.23
  444.5 128.3 %psum.30 = f32[128]{0:T(128)S(1)} all-reduce(f32[128]{0:T(128)S(1)} %multiply_reduce_fusion), channel_id=1, replica_groups=mesh['coarse'=16,'sub'=64] {'coarse','sub'}, use_global_device_ids=true, to_apply=%region_11.13 | all-reduce | flops 128 | bytes 1024 | tf_op jit(solution)/shard_map/psum | solution.py:53
  572.9 0.7 convolution_multiply_fusion
  573.7 6.3 collective-permute-start.24
  580.0 1.9 collective-permute-start.25
  582.0 1.3 collective-permute-start.26
  583.3 1.3 collective-permute-start.27
  584.6 6.4 collective-permute-start.28
  591.1 1.3 collective-permute-start.29
  592.4 1.6 collective-permute-done.25
  594.0 2.0 collective-permute-done.29
  596.1 129.5 %psum.31 = f32[128]{0:T(128)S(1)} all-reduce(f32[128]{0:T(128)S(1)} %fusion.7), channel_id=1, replica_groups=mesh['coarse'=16,'sub'=64] {'coarse','sub'}, use_global_device_ids=true, to_apply=%region_13.15 | all-reduce | flops 128 | bytes 1024 | tf_op jit(solution)/shard_map/psum | solution.py:53
  725.7 0.9 multiply_subtract_fusion
  (161 shorter events, 11.6 us)
Async XLA Ops:
  0.6 190.7 %copy-start = (f32[1,32,512]{2,1,0:T(8,128)S(1)}, f32[1,32,512]{2,1,0:T(8,128)}, u32[]{:S(2)}) copy-start(f32[1,32,512]{2,1,0:T(8,128)} %param.11) | copy-start | bytes 196612
  1.5 130.3 %collective-permute-start = (f32[1,64,128]{2,1,0:T(8,128)S(1)}, f32[1,64,128]{2,1,0:T(8,128)S(1)}, u32[]{:S(2)}, u32[]{:S(2)}) collective-permute-start(f32[1,64,128]{2,1,0:T(8,128)S(1)} %get-tuple-element.60), channel_id=1, source_target_pairs={{0,64},{64,128},{128,192},{192,256},{256,320},{320,384},{384,448},... | collective-permute-start | bytes 98312 | tf_op jit(solution)/shard_map/ppermute | solution.py:21
  22.0 111.3 %collective-permute-start.1 = (f32[1,64,128]{2,1,0:T(8,128)S(1)}, f32[1,64,128]{2,1,0:T(8,128)S(1)}, u32[]{:S(2)}, u32[]{:S(2)}) collective-permute-start(f32[1,64,128]{2,1,0:T(8,128)S(1)} %get-tuple-element.59), channel_id=1, source_target_pairs={{64,0},{128,64},{192,128},{256,192},{320,256},{384,320},{448,384},... | collective-permute-start | bytes 98312 | tf_op jit(solution)/shard_map/ppermute | solution.py:23
  23.9 109.4 %collective-permute-start.2 = (f32[1,64,128]{2,1,0:T(8,128)S(1)}, f32[1,64,128]{2,1,0:T(8,128)S(1)}, u32[]{:S(2)}, u32[]{:S(2)}) collective-permute-start(f32[1,64,128]{2,1,0:T(8,128)S(1)} %get-tuple-element.58), channel_id=1, source_target_pairs={{0,1},{1,2},{2,3},{3,4},{4,5},{5,6},{6,7},{7,8},{8,9},{9,10},{10,1... | collective-permute-start | bytes 98312 | tf_op jit(solution)/shard_map/ppermute | solution.py:21
  27.2 106.2 %collective-permute-start.3 = (f32[1,64,128]{2,1,0:T(8,128)S(1)}, f32[1,64,128]{2,1,0:T(8,128)S(1)}, u32[]{:S(2)}, u32[]{:S(2)}) collective-permute-start(f32[1,64,128]{2,1,0:T(8,128)S(1)} %get-tuple-element.57), channel_id=1, source_target_pairs={{1,0},{2,1},{3,2},{4,3},{5,4},{6,5},{7,6},{8,7},{9,8},{10,9},{11,1... | collective-permute-start | bytes 98312 | tf_op jit(solution)/shard_map/ppermute | solution.py:23
  28.5 6.0 copy-start.4
  28.5 104.9 %collective-permute-start.4 = (f32[64,128]{1,0:T(8,128)S(1)}, f32[64,128]{1,0:T(8,128)S(1)}, u32[]{:S(2)}, u32[]{:S(2)}) collective-permute-start(f32[64,128]{1,0:T(8,128)S(1)} %get-tuple-element.56), channel_id=1, source_target_pairs={{0,8},{1,9},{2,10},{3,11},{4,12},{5,13},{6,14},{7,15},{8,16},{9,17... | collective-permute-start | bytes 98312 | tf_op jit(solution)/shard_map/ppermute | solution.py:33
  34.6 1.3 copy-start.3
  131.9 4.8 copy-start.1
  131.9 4.8 collective-permute-start.5
  192.5 12.7 %collective-permute-start.6 = (f32[1,64,128]{2,1,0:T(8,128)S(1)}, f32[1,64,128]{2,1,0:T(8,128)S(1)}, u32[]{:S(2)}, u32[]{:S(2)}) collective-permute-start(f32[1,64,128]{2,1,0:T(8,128)S(1)} %get-tuple-element.54), channel_id=1, source_target_pairs={{0,64},{64,128},{128,192},{192,256},{256,320},{320,384},{384,448},... | collective-permute-start | bytes 98312 | tf_op jit(solution)/shard_map/ppermute | solution.py:21
  194.4 13.9 %collective-permute-start.7 = (f32[1,64,128]{2,1,0:T(8,128)S(1)}, f32[1,64,128]{2,1,0:T(8,128)S(1)}, u32[]{:S(2)}, u32[]{:S(2)}) collective-permute-start(f32[1,64,128]{2,1,0:T(8,128)S(1)} %get-tuple-element.53), channel_id=1, source_target_pairs={{64,0},{128,64},{192,128},{256,192},{320,256},{384,320},{448,384},... | collective-permute-start | bytes 98312 | tf_op jit(solution)/shard_map/ppermute | solution.py:23
  196.8 11.5 %collective-permute-start.8 = (f32[1,64,128]{2,1,0:T(8,128)S(1)}, f32[1,64,128]{2,1,0:T(8,128)S(1)}, u32[]{:S(2)}, u32[]{:S(2)}) collective-permute-start(f32[1,64,128]{2,1,0:T(8,128)S(1)} %get-tuple-element.52), channel_id=1, source_target_pairs={{0,1},{1,2},{2,3},{3,4},{4,5},{5,6},{6,7},{7,8},{8,9},{9,10},{10,1... | collective-permute-start | bytes 98312 | tf_op jit(solution)/shard_map/ppermute | solution.py:21
  198.1 10.3 %collective-permute-start.9 = (f32[1,64,128]{2,1,0:T(8,128)S(1)}, f32[1,64,128]{2,1,0:T(8,128)S(1)}, u32[]{:S(2)}, u32[]{:S(2)}) collective-permute-start(f32[1,64,128]{2,1,0:T(8,128)S(1)} %get-tuple-element.51), channel_id=1, source_target_pairs={{1,0},{2,1},{3,2},{4,3},{5,4},{6,5},{7,6},{8,7},{9,8},{10,9},{11,1... | collective-permute-start | bytes 98312 | tf_op jit(solution)/shard_map/ppermute | solution.py:23
  199.4 9.0 %collective-permute-start.10 = (f32[64,128]{1,0:T(8,128)S(1)}, f32[64,128]{1,0:T(8,128)S(1)}, u32[]{:S(2)}, u32[]{:S(2)}) collective-permute-start(f32[64,128]{1,0:T(8,128)S(1)} %get-tuple-element.50), channel_id=1, source_target_pairs={{0,8},{1,9},{2,10},{3,11},{4,12},{5,13},{6,14},{7,15},{8,16},{9,17... | collective-permute-start | bytes 98312 | tf_op jit(solution)/shard_map/ppermute | solution.py:33
  205.2 8.0 %copy-start.2 = (f32[1,1,384,384]{3,2,1,0:T(8,128)S(1)}, f32[1,1,384,384]{3,2,1,0:T(8,128)}, u32[]{:S(2)}) copy-start(f32[1,1,384,384]{3,2,1,0:T(8,128)} %param.8) | copy-start | bytes 1769476
  205.2 7.8 %collective-permute-start.11 = (f32[64,128]{1,0:T(8,128)S(1)}, f32[64,128]{1,0:T(8,128)S(1)}, u32[]{:S(2)}, u32[]{:S(2)}) collective-permute-start(f32[64,128]{1,0:T(8,128)S(1)} %get-tuple-element.49), channel_id=1, source_target_pairs={{8,0},{9,1},{10,2},{11,3},{12,4},{13,5},{14,6},{15,7},{16,8},{17,9... | collective-permute-start | bytes 98312 | tf_op jit(solution)/shard_map/ppermute | solution.py:33
  213.9 26.8 %collective-permute-start.12 = (f32[1,64,128]{2,1,0:T(8,128)S(1)}, f32[1,64,128]{2,1,0:T(8,128)S(1)}, u32[]{:S(2)}, u32[]{:S(2)}) collective-permute-start(f32[1,64,128]{2,1,0:T(8,128)S(1)} %get-tuple-element.48), channel_id=1, source_target_pairs={{0,64},{64,128},{128,192},{192,256},{256,320},{320,384},{384,448},... | collective-permute-start | bytes 98312 | tf_op jit(solution)/shard_map/ppermute | solution.py:21
  227.8 14.3 %collective-permute-start.13 = (f32[1,64,128]{2,1,0:T(8,128)S(1)}, f32[1,64,128]{2,1,0:T(8,128)S(1)}, u32[]{:S(2)}, u32[]{:S(2)}) collective-permute-start(f32[1,64,128]{2,1,0:T(8,128)S(1)} %get-tuple-element.47), channel_id=1, source_target_pairs={{64,0},{128,64},{192,128},{256,192},{320,256},{384,320},{448,384},... | collective-permute-start | bytes 98312 | tf_op jit(solution)/shard_map/ppermute | solution.py:23
  229.7 12.4 %collective-permute-start.14 = (f32[1,64,128]{2,1,0:T(8,128)S(1)}, f32[1,64,128]{2,1,0:T(8,128)S(1)}, u32[]{:S(2)}, u32[]{:S(2)}) collective-permute-start(f32[1,64,128]{2,1,0:T(8,128)S(1)} %get-tuple-element.46), channel_id=1, source_target_pairs={{0,1},{1,2},{2,3},{3,4},{4,5},{5,6},{6,7},{7,8},{8,9},{9,10},{10,1... | collective-permute-start | bytes 98312 | tf_op jit(solution)/shard_map/ppermute | solution.py:21
  231.0 11.1 %collective-permute-start.15 = (f32[1,64,128]{2,1,0:T(8,128)S(1)}, f32[1,64,128]{2,1,0:T(8,128)S(1)}, u32[]{:S(2)}, u32[]{:S(2)}) collective-permute-start(f32[1,64,128]{2,1,0:T(8,128)S(1)} %get-tuple-element.45), channel_id=1, source_target_pairs={{1,0},{2,1},{3,2},{4,3},{5,4},{6,5},{7,6},{8,7},{9,8},{10,9},{11,1... | collective-permute-start | bytes 98312 | tf_op jit(solution)/shard_map/ppermute | solution.py:23
  232.3 9.9 %collective-permute-start.16 = (f32[64,128]{1,0:T(8,128)S(1)}, f32[64,128]{1,0:T(8,128)S(1)}, u32[]{:S(2)}, u32[]{:S(2)}) collective-permute-start(f32[64,128]{1,0:T(8,128)S(1)} %get-tuple-element.44), channel_id=1, source_target_pairs={{0,8},{1,9},{2,10},{3,11},{4,12},{5,13},{6,14},{7,15},{8,16},{9,17... | collective-permute-start | bytes 98312 | tf_op jit(solution)/shard_map/ppermute | solution.py:33
  240.7 4.7 collective-permute-start.17
  422.0 17.7 %collective-permute-start.18 = (f32[1,64,128]{2,1,0:T(8,128)S(1)}, f32[1,64,128]{2,1,0:T(8,128)S(1)}, u32[]{:S(2)}, u32[]{:S(2)}) collective-permute-start(f32[1,64,128]{2,1,0:T(8,128)S(1)} %get-tuple-element.42), channel_id=1, source_target_pairs={{0,64},{64,128},{128,192},{192,256},{256,320},{320,384},{384,448},... | collective-permute-start | bytes 98312 | tf_op jit(solution)/shard_map/ppermute | solution.py:21
  427.8 14.0 %collective-permute-start.19 = (f32[1,64,128]{2,1,0:T(8,128)S(1)}, f32[1,64,128]{2,1,0:T(8,128)S(1)}, u32[]{:S(2)}, u32[]{:S(2)}) collective-permute-start(f32[1,64,128]{2,1,0:T(8,128)S(1)} %get-tuple-element.41), channel_id=1, source_target_pairs={{64,0},{128,64},{192,128},{256,192},{320,256},{384,320},{448,384},... | collective-permute-start | bytes 98312 | tf_op jit(solution)/shard_map/ppermute | solution.py:23
  429.8 12.0 %collective-permute-start.20 = (f32[1,64,128]{2,1,0:T(8,128)S(1)}, f32[1,64,128]{2,1,0:T(8,128)S(1)}, u32[]{:S(2)}, u32[]{:S(2)}) collective-permute-start(f32[1,64,128]{2,1,0:T(8,128)S(1)} %get-tuple-element.40), channel_id=1, source_target_pairs={{0,1},{1,2},{2,3},{3,4},{4,5},{5,6},{6,7},{7,8},{8,9},{9,10},{10,1... | collective-permute-start | bytes 98312 | tf_op jit(solution)/shard_map/ppermute | solution.py:21
  431.1 10.8 %collective-permute-start.21 = (f32[1,64,128]{2,1,0:T(8,128)S(1)}, f32[1,64,128]{2,1,0:T(8,128)S(1)}, u32[]{:S(2)}, u32[]{:S(2)}) collective-permute-start(f32[1,64,128]{2,1,0:T(8,128)S(1)} %get-tuple-element.39), channel_id=1, source_target_pairs={{1,0},{2,1},{3,2},{4,3},{5,4},{6,5},{7,6},{8,7},{9,8},{10,9},{11,1... | collective-permute-start | bytes 98312 | tf_op jit(solution)/shard_map/ppermute | solution.py:23
  432.4 9.5 %collective-permute-start.22 = (f32[64,128]{1,0:T(8,128)S(1)}, f32[64,128]{1,0:T(8,128)S(1)}, u32[]{:S(2)}, u32[]{:S(2)}) collective-permute-start(f32[64,128]{1,0:T(8,128)S(1)} %get-tuple-element.38), channel_id=1, source_target_pairs={{0,8},{1,9},{2,10},{3,11},{4,12},{5,13},{6,14},{7,15},{8,16},{9,17... | collective-permute-start | bytes 98312 | tf_op jit(solution)/shard_map/ppermute | solution.py:33
  439.7 4.7 collective-permute-start.23
  573.7 17.4 %collective-permute-start.24 = (f32[1,64,128]{2,1,0:T(8,128)S(1)}, f32[1,64,128]{2,1,0:T(8,128)S(1)}, u32[]{:S(2)}, u32[]{:S(2)}) collective-permute-start(f32[1,64,128]{2,1,0:T(8,128)S(1)} %get-tuple-element.36), channel_id=1, source_target_pairs={{0,64},{64,128},{128,192},{192,256},{256,320},{320,384},{384,448},... | collective-permute-start | bytes 98312 | tf_op jit(solution)/shard_map/ppermute | solution.py:21
  580.0 13.9 %collective-permute-start.25 = (f32[1,64,128]{2,1,0:T(8,128)S(1)}, f32[1,64,128]{2,1,0:T(8,128)S(1)}, u32[]{:S(2)}, u32[]{:S(2)}) collective-permute-start(f32[1,64,128]{2,1,0:T(8,128)S(1)} %get-tuple-element.35), channel_id=1, source_target_pairs={{64,0},{128,64},{192,128},{256,192},{320,256},{384,320},{448,384},... | collective-permute-start | bytes 98312 | tf_op jit(solution)/shard_map/ppermute | solution.py:23
  582.0 12.0 %collective-permute-start.26 = (f32[1,64,128]{2,1,0:T(8,128)S(1)}, f32[1,64,128]{2,1,0:T(8,128)S(1)}, u32[]{:S(2)}, u32[]{:S(2)}) collective-permute-start(f32[1,64,128]{2,1,0:T(8,128)S(1)} %get-tuple-element.34), channel_id=1, source_target_pairs={{0,1},{1,2},{2,3},{3,4},{4,5},{5,6},{6,7},{7,8},{8,9},{9,10},{10,1... | collective-permute-start | bytes 98312 | tf_op jit(solution)/shard_map/ppermute | solution.py:21
  583.3 10.7 %collective-permute-start.27 = (f32[1,64,128]{2,1,0:T(8,128)S(1)}, f32[1,64,128]{2,1,0:T(8,128)S(1)}, u32[]{:S(2)}, u32[]{:S(2)}) collective-permute-start(f32[1,64,128]{2,1,0:T(8,128)S(1)} %get-tuple-element.33), channel_id=1, source_target_pairs={{1,0},{2,1},{3,2},{4,3},{5,4},{6,5},{7,6},{8,7},{9,8},{10,9},{11,1... | collective-permute-start | bytes 98312 | tf_op jit(solution)/shard_map/ppermute | solution.py:23
  584.6 9.5 %collective-permute-start.28 = (f32[64,128]{1,0:T(8,128)S(1)}, f32[64,128]{1,0:T(8,128)S(1)}, u32[]{:S(2)}, u32[]{:S(2)}) collective-permute-start(f32[64,128]{1,0:T(8,128)S(1)} %get-tuple-element.32), channel_id=1, source_target_pairs={{0,8},{1,9},{2,10},{3,11},{4,12},{5,13},{6,14},{7,15},{8,16},{9,17... | collective-permute-start | bytes 98312 | tf_op jit(solution)/shard_map/ppermute | solution.py:33
  591.1 4.9 collective-permute-start.29
where the time goes:
time: 728 us; the launch traced here: 727 us
  blocking collectives  481 us (66%)
  starting transfers between devices  114 us (16%)
  other arithmetic  88.2 us (12%)
  waiting for transfers between devices  19.5 us (3%)
  matrix products  11 us (2%)
  local copies, waits for them, and re-layouts  8.86 us (1%)
    psum x3, blocking collectives, single_sum(): return lax.psum(partial_terms, ('coarse', 'sub'))  388 us
    all_gather x2, blocking collectives, precondition(): lax.all_gather(restricted, 'coarse', axis=0, tiled=True)  93.5 us
    ppermute x10, starting transfers between devices, padded(): lax.ppermute(tail, axis, [(i, (i + 1) % count) for i in range(ends)])  56.5 us
    another operation x10, other arithmetic, on_device(): factor = jnp.linalg.cholesky(operator + matmul(basis_local, basis_local.T))  56.3 us
    ppermute x10, starting transfers between devices, shifted(): return lax.ppermute(value, axis, pairs)  40.7 us
    another operation x4, other arithmetic, precondition(): local_part = jax.scipy.linalg.cho_solve((factor, True), weighted)  29.5 us
    ppermute x10, starting transfers between devices, padded(): lax.ppermute(head, axis, [((i + 1) % count, i) for i in range(ends)])  16.5 us
    ppermute x10, waiting for transfers between devices, shifted(): return lax.ppermute(value, axis, pairs)  15.6 us
  transfers between devices with their start and end apart: 30, of which 8 were waited for; matrix products, arithmetic and copies ran while one was open for 13% of the time, Pallas kernels for 0%

commit v1 on v0

v1 whole, which is shorter than its diff:
```python
import jax
import jax.numpy as jnp
from jax import lax
from jax.experimental import pallas as pl
from jax.experimental.pallas import tpu as pltpu
from jax.sharding import PartitionSpec as P

ROW = 8
X_COUNT, HALF_COUNT, CORE_COUNT = 4, 2, 2
LOW_COUNT, Y_COUNT = 8, 8
LEAF = 128
GROUP = 8

MESH = pl.DeviceIdType.MESH
highest = lax.Precision.HIGHEST


def dot(former, latter):
    return jnp.dot(former, latter, precision=highest, preferred_element_type=jnp.float32)


def dot_left_transposed(former, latter):
    return lax.dot_general(
        former, latter, (((0,), (0,)), ((), ())), precision=highest, preferred_element_type=jnp.float32
    )


def dot_right_transposed(former, latter):
    return lax.dot_general(
        former, latter, (((1,), (1,)), ((), ())), precision=highest, preferred_element_type=jnp.float32
    )


def reciprocal(value):
    guess = pl.reciprocal(value, approx=True)
    guess = guess * (2.0 - value * guess)
    return guess * (2.0 - value * guess)


def product(former, latter):
    out = []
    for row in former:
        line = []
        for j in range(len(latter[0])):
            total = row[0] * latter[0][j]
            for t in range(1, len(latter)):
                total = total + row[t] * latter[t][j]
            line.append(total)
        out.append(line)
    return out


def small_inverse(matrix):
    size = len(matrix)
    if size == 2:
        a, b, c = matrix[0][0], matrix[0][1], matrix[1][1]
        det = reciprocal(a * c - b * b)
        return [[c * det, -b * det], [-b * det, a * det]]
    half = size // 2
    corner = [row[half:] for row in matrix[:half]]
    first = small_inverse([row[:half] for row in matrix[:half]])
    carried = product(first, corner)
    rest = [[None] * half for _ in range(half)]
    for i in range(half):
        for j in range(i, half):
            total = matrix[half + i][half + j]
            for t in range(half):
                total = total - corner[t][i] * carried[t][j]
            rest[i][j] = rest[j][i] = total
    second = small_inverse(rest)
    side = product(carried, second)
    out = [[None] * size for _ in range(size)]
    for i in range(half):
        for j in range(i, half):
            total = first[i][j]
            for t in range(half):
                total = total + side[i][t] * carried[j][t]
            out[i][j] = out[j][i] = total
        for j in range(half):
            out[i][half + j] = out[half + j][i] = -side[i][j]
            out[half + i][half + j] = second[i][j]
    return out


def invert_leaf(leaf_ref):
    shape = (GROUP, LEAF)
    lane = lax.broadcasted_iota(jnp.int32, shape, 1)
    sublane = lax.broadcasted_iota(jnp.int32, shape, 0)

    def step(g, carry):
        base = pl.multiple_of(g * GROUP, GROUP)
        rows = [jnp.broadcast_to(leaf_ref[pl.ds(base + t, 1), :], shape) for t in range(GROUP)]
        pivots = [[None] * GROUP for _ in range(GROUP)]
        for r in range(GROUP):
            for s in range(r, GROUP):
                pivots[r][s] = pivots[s][r] = jnp.broadcast_to(rows[r][:, s : s + 1], shape)
        inverse = small_inverse(pivots)
        unit = [jnp.where(lane == t, 1.0, jnp.where(lane < GROUP, 0.0, rows[t])) for t in range(GROUP)]
        solved = []
        for s in range(GROUP):
            total = inverse[s][0] * unit[0]
            for t in range(1, GROUP):
                total = total + inverse[s][t] * unit[t]
            solved.append(total)
        tile = solved[0]
        for s in range(1, GROUP):
            tile = jnp.where(sublane == s, solved[s], tile)
        for i in range(LEAF // GROUP):
            place = slice(i * GROUP, (i + 1) * GROUP)
            old = leaf_ref[place, :]
            new = jnp.where(lane < GROUP, 0.0, old)
            for s in range(GROUP):
                new = new - jnp.broadcast_to(old[:, s : s + 1], shape) * solved[s]
            leaf_ref[place, :] = pltpu.roll(jnp.where(g == i, tile, new), LEAF - GROUP, 1)
        return carry

    lax.fori_loop(0, LEAF // GROUP, step, 0)


def invert_in_place(matrix_ref, leaf_ref):
    blocks = matrix_ref.shape[0] // LEAF
    for j in range(blocks):
        here = slice(j * LEAF, (j + 1) * LEAF)
        leaf_ref[...] = matrix_ref[here, here]
        invert_leaf(leaf_ref)
        inverse = leaf_ref[...]
        matrix_ref[here, here] = inverse
        others = [slice(i * LEAF, (i + 1) * LEAF) for i in range(blocks) if i != j]
        for columns in others:
            matrix_ref[here, columns] = dot(inverse, matrix_ref[here, columns])
        for rows in others:
            column = matrix_ref[rows, here]
            for columns in others:
                matrix_ref[rows, columns] = matrix_ref[rows, columns] - dot(column, matrix_ref[here, columns])
            matrix_ref[rows, here] = -dot(column, inverse)


def factor_kernel(schur_ref, basis_ref, scaling_column_ref, scaling_row_ref, operator_ref, inverse_ref, leaf_ref):
    operator = scaling_column_ref[...] * schur_ref[...] * scaling_row_ref[...]
    operator_ref[...] = operator
    basis = basis_ref[...]
    inverse_ref[...] = operator + dot_right_transposed(basis, basis)
    invert_in_place(inverse_ref, leaf_ref)


def make_iterate_kernel(sizes):
    x_count, half_count, core_count, low_count, y_count, row_step = sizes
    coarse_count = x_count * half_count * core_count
    sub_count = low_count * y_count
    near_count = x_count * core_count
    far_count = low_count * half_count

    def kernel(
        loads_ref, operator_ref, inverse_ref, basis_ref, rows_ref, solution_ref, residual_ref,
        halo, unsummed, gathered, partner_rows, part, part_in, sums_a, sums_b, sums_c,
        halo_send, halo_recv, near_send, near_recv, pair_send, pair_recv,
        a_send, a_recv, b_send, b_recv, c_send, c_recv,
    ):
        faces, dofs, cases = loads_ref.shape
        order = faces * dofs
        width = basis_ref.shape[1]
        coarse = lax.axis_index("coarse")
        sub = lax.axis_index("sub")
        core = coarse % core_count
        half = (coarse // core_count) % half_count
        x = coarse // (core_count * half_count)
        y = sub % y_count
        low = sub // y_count
        near = x * core_count + core
        far = low * half_count + half

        def near_device(index):
            return ((index // core_count * half_count + half) * core_count + index % core_count, sub)

        def y_device(index):
            return (coarse, low * y_count + index)

        def far_device(index):
            return ((x * half_count + index % half_count) * core_count + core, index // half_count * y_count + y)

        partner = ((x * half_count + (half_count - 1 - half)) * core_count + core, sub)
        present = [
            coarse > 0,
            coarse < coarse_count - 1,
            sub > 0,
            sub < sub_count - 1,
            sub >= row_step,
            sub < sub_count - row_step,
        ]
        neighbour = [
            (coarse - 1, sub),
            (coarse + 1, sub),
            (coarse, sub - 1),
            (coarse, sub + 1),
            (coarse, sub - row_step),
            (coarse, sub + row_step),
        ]

        barrier = pltpu.get_barrier_semaphore()

        def greet(device):
            pl.semaphore_signal(barrier, inc=1, device_id=device, device_id_type=MESH)

        lax.fori_loop(1, near_count, lambda j, c: (greet(near_device((near + j) % near_count)), c)[1], 0)
        lax.fori_loop(1, y_count, lambda j, c: (greet(y_device((y + j) % y_count)), c)[1], 0)
        lax.fori_loop(1, far_count, lambda j, c: (greet(far_device((far + j) % far_count)), c)[1], 0)
        expected = near_count + y_count + far_count - 3
        for face in range(faces):
            expected = expected + present[face].astype(jnp.int32)

            @pl.when(present[face])
            def _():
                greet(neighbour[face])

        weights = [jnp.where(present[face], 0.5, 1.0) for face in range(faces)]
        for face in range(faces):

            @pl.when(jnp.logical_not(present[face]))
            def _():
                for k in range(halo.shape[0]):
                    halo[k, face] = jnp.zeros((dofs, cases), jnp.float32)

        for k in range(gathered.shape[0]):
            for index in range(near_count):
                place = (index // core_count * half_count + (half_count - 1 - half)) * core_count + index % core_count
                gathered[k, place] = jnp.zeros(gathered.shape[2:], jnp.float32)
        pl.semaphore_wait(barrier, expected)

        def halo_copy(k, source, face):
            return pltpu.make_async_remote_copy(
                src_ref=source.at[face],
                dst_ref=halo.at[k, face ^ 1],
                send_sem=halo_send.at[k, face],
                recv_sem=halo_recv.at[k, face ^ 1],
                device_id=neighbour[face],
                device_id_type=MESH,
            )

        def halo_start(k, source):
            for face in range(faces):

                @pl.when(present[face])
                def _():
                    halo_copy(k, source, face).start()

        def halo_wait(k, source):
            for face in range(faces):

                @pl.when(present[face])
                def _():
                    halo_copy(k, source, face ^ 1).wait_recv()

        def halo_finish(k, source):
            for face in range(faces):

                @pl.when(present[face])
                def _():
                    halo_copy(k, source, face).wait_send()

        def pair_copy(k, source, target):
            return pltpu.make_async_remote_copy(
                src_ref=source,
                dst_ref=target,
                send_sem=pair_send.at[k],
                recv_sem=pair_recv.at[k],
                device_id=partner,
                device_id_type=MESH,
            )

        def spread_copy(buffer, send, recv, k, mine, device, slot, index):
            return pltpu.make_async_remote_copy(
                src_ref=buffer.at[k, mine],
                dst_ref=buffer.at[k, slot],
                send_sem=send.at[k, index],
                recv_sem=recv.at[k, slot],
                device_id=device,
                device_id_type=MESH,
            )

        def spread_start(buffer, send, recv, k, mine, count, device_of):
            def body(j, carry):
                index = (mine + j) % count
                spread_copy(buffer, send, recv, k, mine, device_of(index), mine, index).start()
                return carry

            lax.fori_loop(1, count, body, 0)

        def spread_wait(buffer, send, recv, k, mine, count, device_of):
            def body(j, carry):
                index = (mine + j) % count
                spread_copy(buffer, send, recv, k, mine, device_of(index), index, index).wait_recv()
                return carry

            lax.fori_loop(1, count, body, 0)

        def spread_finish(buffer, send, recv, k, mine, count, device_of):
            def body(j, carry):
                index = (mine + j) % count
                spread_copy(buffer, send, recv, k, mine, device_of(index), mine, index).wait_send()
                return carry

            lax.fori_loop(1, count, body, 0)

        stages = [
            (sums_a, a_send, a_recv, near, near_count, near_device),
            (sums_b, b_send, b_recv, y, y_count, y_device),
            (sums_c, c_send, c_recv, far, far_count, far_device),
        ]

        def sum_start(k, stage, value):
            buffer, send, recv, mine, count, device_of = stages[stage]
            buffer[k, mine] = value
            spread_start(buffer, send, recv, k, mine, count, device_of)

        def sum_end(k, stage):
            buffer, send, recv, mine, count, device_of = stages[stage]
            spread_wait(buffer, send, recv, k, mine, count, device_of)
            total = buffer[k, 0]
            for index in range(1, count):
                total = total + buffer[k, index]
            return total

        def weigh(vector):
            pieces = [vector[face * dofs : (face + 1) * dofs] * weights[face] for face in range(faces)]
            return jnp.concatenate(pieces, axis=0)

        def gather_start(k, weighted):
            gathered[k, coarse] = dot_left_transposed(basis_ref[...], weighted)

            def body(j, carry):
                index = (near + j) % near_count
                spread_copy(gathered, near_send, near_recv, k, coarse, near_device(index), coarse, index).start()
                return carry

            lax.fori_loop(1, near_count, body, 0)

        def gather_wait(k):
            def body(j, carry):
                index = (near + j) % near_count
                device = near_device(index)
                spread_copy(gathered, near_send, near_recv, k, coarse, device, device[0], index).wait_recv()
                return carry

            lax.fori_loop(1, near_count, body, 0)

        def gather_finish(k):
            def body(j, carry):
                index = (near + j) % near_count
                spread_copy(gathered, near_send, near_recv, k, coarse, near_device(index), coarse, index).wait_send()
                return carry

            lax.fori_loop(1, near_count, body, 0)

        def precondition(k, vector, target):
            weighted = weigh(vector)
            gather_start(k, weighted)
            solved = dot(inverse_ref[...], weighted)
            if k == 0:
                pair_copy(2, rows_ref, partner_rows).wait_recv()
            gather_wait(k)
            stacked = gathered[k].reshape(coarse_count * width, cases)
            part[k] = dot(partner_rows[...], stacked)
            pair = pair_copy(k, part.at[k], part_in.at[k])
            pair.start()
            own = dot(rows_ref[...], stacked)
            pair.wait_recv()
            combined = weigh(solved + dot(basis_ref[...], own + part_in[k]))
            target[...] = combined.reshape(faces, dofs, cases)
            return combined

        def column_sum(value):
            return jnp.sum(value, axis=0, keepdims=True)

        def flat(ref):
            return ref[...].reshape(order, cases)

        halo_start(0, loads_ref)
        pair_copy(2, rows_ref, partner_rows).start()
        halo_wait(0, loads_ref)
        r0 = flat(loads_ref) + flat(halo.at[0])
        u0 = precondition(0, r0, unsummed.at[0])
        halo_start(1, unsummed.at[0])
        gamma_part = column_sum(r0 * u0)
        halo_wait(1, unsummed.at[0])
        z0 = u0 + flat(halo.at[1])
        t0 = dot(operator_ref[...], z0)
        unsummed[1] = t0.reshape(faces, dofs, cases)
        halo_start(2, unsummed.at[1])
        pad = jnp.zeros((5, cases), jnp.float32)
        sum_start(0, 0, jnp.concatenate([gamma_part, column_sum(z0 * t0), pad, pad[:1]], axis=0))
        halo_wait(2, unsummed.at[1])
        q0 = t0 + flat(halo.at[2])
        sum_start(0, 1, sum_end(0, 0))
        u1 = precondition(1, q0, unsummed.at[2])
        halo_start(3, unsummed.at[2])
        sum_start(0, 2, sum_end(0, 1))
        halo_wait(3, unsummed.at[2])
        w0 = u1 + flat(halo.at[3])
        t1 = dot(operator_ref[...], w0)
        unsummed[3] = t1.reshape(faces, dofs, cases)
        halo_start(4, unsummed.at[3])
        first = sum_end(0, 2)
        gamma, energy = first[0:1], first[1:2]
        step = gamma / energy
        z1 = z0 - step * w0
        r1 = r0 - step * q0
        t1 = t0 - step * t1
        sum_start(
            1,
            0,
            jnp.concatenate(
                [column_sum(r1 * (u0 - step * u1)), column_sum(z1 * t1), column_sum(z0 * t1), pad], axis=0
            ),
        )
        sum_start(1, 1, sum_end(1, 0))
        sum_start(1, 2, sum_end(1, 1))
        halo_wait(4, unsummed.at[3])
        mapped = t1 + flat(halo.at[2]) - step * flat(halo.at[4])
        second = sum_end(1, 2)
        gamma_next = second[0:1]
        ratio = gamma_next / gamma
        last = gamma_next / (second[1:2] + 2.0 * ratio * second[2:3] + ratio * ratio * energy)
        solution_ref[...] = (step * z0 + last * (z1 + ratio * z0)).reshape(faces, dofs, cases)
        residual_ref[...] = (r1 - last * (mapped + ratio * q0)).reshape(faces, dofs, cases)

        halo_finish(0, loads_ref)
        for k in range(1, 5):
            halo_finish(k, unsummed.at[k - 1])
        pair_copy(2, rows_ref, partner_rows).wait_send()
        for k in range(2):
            gather_finish(k)
            pair_copy(k, part.at[k], part_in.at[k]).wait_send()
            for buffer, send, recv, mine, count, device_of in stages:
                spread_finish(buffer, send, recv, k, mine, count, device_of)

    return kernel


def in_vmem(count):
    return [pl.BlockSpec(memory_space=pltpu.VMEM)] * count


def on_device(sizes, face_loads, schur_blocks, coarse_basis, drop_masks, coarse_inverse):
    x_count, half_count, core_count, low_count, y_count, row_step = sizes
    coarse_count = x_count * half_count * core_count
    near_count, far_count = x_count * core_count, low_count * half_count
    faces, dofs, cases = face_loads.shape[2:]
    order = faces * dofs
    width = coarse_basis.shape[3]
    square = jax.ShapeDtypeStruct((order, order), jnp.float32)
    scaling = 1.0 + drop_masks.astype(jnp.float32)
    operator, inverse = pl.pallas_call(
        factor_kernel,
        out_shape=[square, square],
        in_specs=in_vmem(4),
        out_specs=in_vmem(2),
        scratch_shapes=[pltpu.VMEM((LEAF, LEAF), jnp.float32)],
        compiler_params=pltpu.CompilerParams(vmem_limit_bytes=16 << 20),
    )(schur_blocks[0, 0], coarse_basis[0, 0], scaling.reshape(order, 1), scaling.reshape(1, order))
    vector = jax.ShapeDtypeStruct((faces, dofs, cases), jnp.float32)
    dma = pltpu.SemaphoreType.DMA
    solved, residual = pl.pallas_call(
        make_iterate_kernel(sizes),
        out_shape=[vector, vector],
        in_specs=in_vmem(5),
        out_specs=in_vmem(2),
        scratch_shapes=[
            pltpu.VMEM((5, faces, dofs, cases), jnp.float32),
            pltpu.VMEM((4, faces, dofs, cases), jnp.float32),
            pltpu.VMEM((2, coarse_count, width, cases), jnp.float32),
            pltpu.VMEM((width, coarse_count * width), jnp.float32),
            pltpu.VMEM((2, width, cases), jnp.float32),
            pltpu.VMEM((2, width, cases), jnp.float32),
            pltpu.VMEM((2, near_count, 8, cases), jnp.float32),
            pltpu.VMEM((2, y_count, 8, cases), jnp.float32),
            pltpu.VMEM((2, far_count, 8, cases), jnp.float32),
            dma((5, faces)),
            dma((5, faces)),
            dma((2, near_count)),
            dma((2, coarse_count)),
            dma((3,)),
            dma((3,)),
            dma((2, near_count)),
            dma((2, near_count)),
            dma((2, y_count)),
            dma((2, y_count)),
            dma((2, far_count)),
            dma((2, far_count)),
        ],
        compiler_params=pltpu.CompilerParams(
            collective_id=0, has_side_effects=True, vmem_limit_bytes=32 << 20
        ),
    )(face_loads[0, 0], operator, inverse, coarse_basis[0, 0], coarse_inverse[0])
    return solved[None, None], residual[None, None]


def solution(mesh, sizes=(X_COUNT, HALF_COUNT, CORE_COUNT, LOW_COUNT, Y_COUNT, ROW)):
    def body(*arrays):
        return on_device(sizes, *arrays)

    return jax.shard_map(
        body,
        mesh=mesh,
        in_specs=(
            P("coarse", "sub", None, None, None),
            P("coarse", "sub", None, None),
            P("coarse", "sub", None, None),
            P("coarse", "sub", None, None),
            P("sub", "coarse", None),
        ),
        out_specs=(P("coarse", "sub", None, None, None), P("coarse", "sub", None, None, None)),
        check_vma=False,
    )
```

time: 728 us -> 135 us (0.19)
  blocking collectives: 481 us -> 0 us
  Pallas kernels: 0 us -> 130 us
  starting transfers between devices: 114 us -> 0 us
  other arithmetic: 88.2 us -> 0.02 us
  waiting for transfers between devices: 19.5 us -> 0 us
  matrix products: 11 us -> 0 us
    psum x3 -> x0, blocking collectives: 388 us -> none  [single_sum(): return lax.psum(partial_terms, ('coarse', 'sub'))]
    pallas_call x0 -> x2, Pallas kernels: none -> 130 us  [the longest x1 105 us: on_device(): pl.pallas_call(make_iterate_kernel(sizes), out_shape=[vector, vector], in...]
    ppermute x30 -> x0, starting transfers between devices: 114 us -> none  [the longest x10 56.5 us: padded(): lax.ppermute(tail, axis, [(i, (i + 1) % count) for i in range(ends)])]
    all_gather x2 -> x0, blocking collectives: 93.5 us -> none  [precondition(): lax.all_gather(restricted, 'coarse', axis=0, tiled=True)]
    another operation x14 -> x0, other arithmetic: 85.9 us -> none  [the longest x10 56.3 us: on_device(): factor = jnp.linalg.cholesky(operator + matmul(basis_local, basis_local.T))]
    ppermute x30 -> x0, waiting for transfers between devices: 19.5 us -> none  [the longest x10 15.6 us: shifted(): return lax.ppermute(value, axis, pairs)]
  transfers between devices with their start and end apart: 30 -> 0, of which waited for: 8 -> 0; matrix products, arithmetic and copies ran while one was open for 13% -> 0% of each run, Pallas kernels for 0% -> 0%
where the time goes in v1:
time: 135 us
  Pallas kernels  130 us (96%)
  local copies, waits for them, and re-layouts  4.09 us (3%)
    pallas_call x1, Pallas kernels, on_device(): pl.pallas_call(make_iterate_kernel(sizes), out_shape=[vector, vector], in...  105 us
    pallas_call x1, Pallas kernels, on_device(): pl.pallas_call(factor_kernel, out_shape=[square, square], in_specs=in_vme...  25.3 us
    unnamed x13, local copies, waits for them, and re-layouts  3.85 us

profile of v1, /device:TPU:1, one launch (start us, length us, event | category | flops | bytes accessed | tf_op | source)
XLA Modules:
  0.0 135.1 jit_solution(3668878357857732124)
XLA Ops:
  0.6 0.0 copy-start.4
  0.6 0.7 copy-done.4
  1.3 0.1 reshape.11.scaling_row_ref
  1.4 0.0 copy-start.3
  1.4 0.2 reshape.12.scaling_column_ref
  1.6 0.6 copy-done.3
  2.2 0.1 copy.8
  2.3 0.0 copy-start
  2.4 1.1 copy-done
  3.4 0.0 copy-start.1
  3.4 0.0 copy-start.2
  3.4 25.3 %shard_map.68 = (f32[384,384]{1,0:T(8,128)S(1)}, f32[384,384]{1,0:T(8,128)S(1)}) custom-call(f32[384,384]{1,0:T(8,128)S(1)} %bitcast.8, f32[384,32]{1,0:T(8,128)S(1)} %bitcast.6, f32[384,1]{1,0:T(8,128)S(1)} %reshape.12.scaling_column_ref, f32[1,384]{1,0:T(1,128)S(1)} %reshape.11.scaling_row_ref), custom_call_target="tpu_custom_call" | custom-call | tf_op jit(solution)/shard_map/pallas_call | solution.py:452
  28.7 0.0 copy-done.1
  28.8 0.0 copy-done.2
  28.8 104.9 %shard_map.69 = (f32[6,64,128]{2,1,0:T(8,128)S(1)}, f32[6,64,128]{2,1,0:T(8,128)S(1)}) custom-call(f32[6,64,128]{2,1,0:T(8,128)S(1)} %bitcast.9, f32[384,384]{1,0:T(8,128)S(1)} %get-tuple-element.6.operator_ref, f32[384,384]{1,0:T(8,128)S(1)} %get-tuple-element.7.inverse_ref, f32[384,32]{1,0:T(8,128)S(1)} %bitcast.7, f32[32,512]{1,0:T(8,128)S(1)} %bitcast.12), custom_call_target="tpu_custom_call" | custom-call | tf_op jit(solution)/shard_map/pallas_call | solution.py:462
  133.7 0.7 copy.12
  134.4 0.7 copy.13
  (1 shorter events, 0.0 us)
Async XLA Ops:
  0.6 0.7 copy-start.4
  1.4 0.8 copy-start.3
  2.3 1.1 copy-start
  3.4 25.3 %copy-start.1 = (f32[1,1,6,64,128]{4,3,2,1,0:T(8,128)S(1)}, f32[1,1,6,64,128]{4,3,2,1,0:T(8,128)}, u32[]{:S(2)}) copy-start(f32[1,1,6,64,128]{4,3,2,1,0:T(8,128)} %param.5) | copy-start | bytes 589828
  3.4 25.3 %copy-start.2 = (f32[1,32,512]{2,1,0:T(8,128)S(1)}, f32[1,32,512]{2,1,0:T(8,128)}, u32[]{:S(2)}) copy-start(f32[1,32,512]{2,1,0:T(8,128)} %param.9) | copy-start | bytes 196612

commit v2 on v1

--- a/solution.py
+++ b/solution.py
@@ -33,7 +33,6 @@
 
 def reciprocal(value):
     guess = pl.reciprocal(value, approx=True)
-    guess = guess * (2.0 - value * guess)
     return guess * (2.0 - value * guess)
 
 
@@ -82,65 +81,77 @@
     return out
 
 
-def invert_leaf(leaf_ref):
+def invert_leaf(leaf_ref, panel_ref, entry_ref):
     shape = (GROUP, LEAF)
     lane = lax.broadcasted_iota(jnp.int32, shape, 1)
     sublane = lax.broadcasted_iota(jnp.int32, shape, 0)
-
-    def step(g, carry):
-        base = pl.multiple_of(g * GROUP, GROUP)
-        rows = [jnp.broadcast_to(leaf_ref[pl.ds(base + t, 1), :], shape) for t in range(GROUP)]
+    wide_lane = lax.broadcasted_iota(jnp.int32, (LEAF, LEAF), 1)
+    last = LEAF - GROUP
+
+    def solve(panel):
+        for s in range(GROUP):
+            entry_ref[s] = jnp.broadcast_to(panel[:, s : s + 1], shape)
         pivots = [[None] * GROUP for _ in range(GROUP)]
         for r in range(GROUP):
             for s in range(r, GROUP):
-                pivots[r][s] = pivots[s][r] = jnp.broadcast_to(rows[r][:, s : s + 1], shape)
+                pivots[r][s] = pivots[s][r] = jnp.broadcast_to(entry_ref[s, r : r + 1, :], shape)
         inverse = small_inverse(pivots)
-        unit = [jnp.where(lane == t, 1.0, jnp.where(lane < GROUP, 0.0, rows[t])) for t in range(GROUP)]
+        turned = jnp.where(lane >= last, 0.0, pltpu.roll(panel, last, 1))
+        panel_ref[...] = jnp.where(lane == last + sublane, 1.0, turned)
+        unit = [jnp.broadcast_to(panel_ref[t : t + 1, :], shape) for t in range(GROUP)]
         solved = []
         for s in range(GROUP):
             total = inverse[s][0] * unit[0]
             for t in range(1, GROUP):
                 total = total + inverse[s][t] * unit[t]
             solved.append(total)
+        return solved
+
+    def tile_of(solved):
         tile = solved[0]
         for s in range(1, GROUP):
             tile = jnp.where(sublane == s, solved[s], tile)
+        return tile
+
+    def update(tile):
+        old = leaf_ref[...]
+        turned = jnp.where(wide_lane >= last, 0.0, pltpu.roll(old, last, 1))
+        return turned - dot(old[:, :GROUP], tile)
+
+    def step(g, solved):
+        tile = tile_of(solved)
+        old = leaf_ref[pl.ds(pl.multiple_of((g + 1) * GROUP, GROUP), GROUP), :]
+        panel = jnp.where(lane >= last, 0.0, pltpu.roll(old, last, 1))
+        for s in range(GROUP):
+            panel = panel - jnp.broadcast_to(old[:, s : s + 1], shape) * solved[s]
+        following = solve(panel)
+        new = update(tile)
         for i in range(LEAF // GROUP):
-            place = slice(i * GROUP, (i + 1) * GROUP)
-            old = leaf_ref[place, :]
-            new = jnp.where(lane < GROUP, 0.0, old)
-            for s in range(GROUP):
-                new = new - jnp.broadcast_to(old[:, s : s + 1], shape) * solved[s]
-            leaf_ref[place, :] = pltpu.roll(jnp.where(g == i, tile, new), LEAF - GROUP, 1)
-        return carry
-
-    lax.fori_loop(0, LEAF // GROUP, step, 0)
-
-
-def invert_in_place(matrix_ref, leaf_ref):
+            rows = slice(i * GROUP, (i + 1) * GROUP)
+            leaf_ref[rows, :] = jnp.where(g == i, tile, jnp.where(g + 1 == i, panel, new[rows]))
+        return following
+
+    solved = lax.fori_loop(0, LEAF // GROUP - 1, step, solve(leaf_ref[:GROUP, :]))
+    new = update(tile_of(solved))
+    leaf_ref[:last, :] = new[:last]
+    leaf_ref[last:, :] = tile_of(solved)
+
+
+def eliminate(matrix_ref, leaf_ref, panel_ref, entry_ref, j):
     blocks = matrix_ref.shape[0] // LEAF
-    for j in range(blocks):
-        here = slice(j * LEAF, (j + 1) * LEAF)
-        leaf_ref[...] = matrix_ref[here, here]
-        invert_leaf(leaf_ref)
-        inverse = leaf_ref[...]
-        matrix_ref[here, here] = inverse
-        others = [slice(i * LEAF, (i + 1) * LEAF) for i in range(blocks) if i != j]
+    here = slice(j * LEAF, (j + 1) * LEAF)
+    leaf_ref[...] = matrix_ref[here, here]
+    invert_leaf(leaf_ref, panel_ref, entry_ref)
+    inverse = leaf_ref[...]
+    matrix_ref[here, here] = inverse
+    others = [slice(i * LEAF, (i + 1) * LEAF) for i in range(blocks) if i != j]
+    for columns in others:
+        matrix_ref[here, columns] = dot(inverse, matrix_ref[here, columns])
+    for rows in others:
+        column = matrix_ref[rows, here]
         for columns in others:
-            matrix_ref[here, columns] = dot(inverse, matrix_ref[here, columns])
-        for rows in others:
-            column = matrix_ref[rows, here]
-            for columns in others:
-                matrix_ref[rows, columns] = matrix_ref[rows, columns] - dot(column, matrix_ref[here, columns])
-            matrix_ref[rows, here] = -dot(column, inverse)
-
-
-def factor_kernel(schur_ref, basis_ref, scaling_column_ref, scaling_row_ref, operator_ref, inverse_ref, leaf_ref):
-    operator = scaling_column_ref[...] * schur_ref[...] * scaling_row_ref[...]
-    operator_ref[...] = operator
-    basis = basis_ref[...]
-    inverse_ref[...] = operator + dot_right_transposed(basis, basis)
-    invert_in_place(inverse_ref, leaf_ref)
+            matrix_ref[rows, columns] = matrix_ref[rows, columns] - dot(column, matrix_ref[here, columns])
+        matrix_ref[rows, here] = -dot(column, inverse)
 
 
 def make_iterate_kernel(sizes):
@@ -151,8 +162,10 @@
     far_count = low_count * half_count
 
     def kernel(
-        loads_ref, operator_ref, inverse_ref, basis_ref, rows_ref, solution_ref, residual_ref,
-        halo, unsummed, gathered, partner_rows, part, part_in, sums_a, sums_b, sums_c,
+        loads_hbm, schur_hbm, basis_hbm, masks_ref, rows_hbm, solution_ref, residual_ref,
+        loads_ref, operator_ref, basis_ref, rows_ref, inverse_ref, leaf_ref, panel_ref, entry_ref,
+        halo, unsummed, gathered, partner_rows, part, part_in, sums_1a, sums_1b, sums_1c, sums_2a, sums_2b, sums_2c,
+        own_sem,
         halo_send, halo_recv, near_send, near_recv, pair_send, pair_recv,
         a_send, a_recv, b_send, b_recv, c_send, c_recv,
     ):
@@ -196,6 +209,13 @@
             (coarse, sub + row_step),
         ]
 
+        own = []
+        for n, (source, target) in enumerate(
+            [(loads_hbm, loads_ref), (schur_hbm, operator_ref), (basis_hbm, basis_ref), (rows_hbm, rows_ref)]
+        ):
+            own.append(pltpu.make_async_copy(source, target, own_sem.at[n]))
+            own[n].start()
+
         barrier = pltpu.get_barrier_semaphore()
 
         def greet(device):
@@ -224,6 +244,8 @@
             for index in range(near_count):
                 place = (index // core_count * half_count + (half_count - 1 - half)) * core_count + index % core_count
                 gathered[k, place] = jnp.zeros(gathered.shape[2:], jnp.float32)
+        own[0].wait()
+        own[3].wait()
         pl.semaphore_wait(barrier, expected)
 
         def halo_copy(k, source, face):
@@ -269,8 +291,8 @@
 
         def spread_copy(buffer, send, recv, k, mine, device, slot, index):
             return pltpu.make_async_remote_copy(
-                src_ref=buffer.at[k, mine],
-                dst_ref=buffer.at[k, slot],
+                src_ref=buffer.at[mine],
+                dst_ref=buffer.at[slot],
                 send_sem=send.at[k, index],
                 recv_sem=recv.at[k, slot],
                 device_id=device,
@@ -302,22 +324,24 @@
             lax.fori_loop(1, count, body, 0)
 
         stages = [
-            (sums_a, a_send, a_recv, near, near_count, near_device),
-            (sums_b, b_send, b_recv, y, y_count, y_device),
-            (sums_c, c_send, c_recv, far, far_count, far_device),
+            ((sums_1a, sums_2a), a_send, a_recv, near, near_count, near_device),
+            ((sums_1b, sums_2b), b_send, b_recv, y, y_count, y_device),
+            ((sums_1c, sums_2c), c_send, c_recv, far, far_count, far_device),
         ]
 
         def sum_start(k, stage, value):
-            buffer, send, recv, mine, count, device_of = stages[stage]
-            buffer[k, mine] = value
+            buffers, send, recv, mine, count, device_of = stages[stage]
+            buffer = buffers[k]
+            buffer[mine] = value
             spread_start(buffer, send, recv, k, mine, count, device_of)
 
         def sum_end(k, stage):
-            buffer, send, recv, mine, count, device_of = stages[stage]
+            buffers, send, recv, mine, count, device_of = stages[stage]
+            buffer = buffers[k]
             spread_wait(buffer, send, recv, k, mine, count, device_of)
-            total = buffer[k, 0]
+            total = buffer[0]
             for index in range(1, count):
-                total = total + buffer[k, index]
+                total = total + buffer[index]
             return total
 
         def weigh(vector):
@@ -329,7 +353,7 @@
 
             def body(j, carry):
                 index = (near + j) % near_count
-                spread_copy(gathered, near_send, near_recv, k, coarse, near_device(index), coarse, index).start()
+                spread_copy(gathered.at[k], near_send, near_recv, k, coarse, near_device(index), coarse, index).start()
                 return carry
 
             lax.fori_loop(1, near_count, body, 0)
@@ -338,7 +362,7 @@
             def body(j, carry):
                 index = (near + j) % near_count
                 device = near_device(index)
-                spread_copy(gathered, near_send, near_recv, k, coarse, device, device[0], index).wait_recv()
+                spread_copy(gathered.at[k], near_send, near_recv, k, coarse, device, device[0], index).wait_recv()
                 return carry
 
             lax.fori_loop(1, near_count, body, 0)
@@ -346,28 +370,27 @@
         def gather_finish(k):
             def body(j, carry):
                 index = (near + j) % near_count
-                spread_copy(gathered, near_send, near_recv, k, coarse, near_device(index), coarse, index).wait_send()
+                spread_copy(gathered.at[k], near_send, near_recv, k, coarse, near_device(index), coarse, index).wait_send()
                 return carry
 
             lax.fori_loop(1, near_count, body, 0)
 
-        def precondition(k, vector, target):
-            weighted = weigh(vector)
-            gather_start(k, weighted)
-            solved = dot(inverse_ref[...], weighted)
-            if k == 0:
-                pair_copy(2, rows_ref, partner_rows).wait_recv()
+        def coarse_start(k):
             gather_wait(k)
             stacked = gathered[k].reshape(coarse_count * width, cases)
             part[k] = dot(partner_rows[...], stacked)
-            pair = pair_copy(k, part.at[k], part_in.at[k])
-            pair.start()
-            own = dot(rows_ref[...], stacked)
-            pair.wait_recv()
-            combined = weigh(solved + dot(basis_ref[...], own + part_in[k]))
+            pair_copy(k, part.at[k], part_in.at[k]).start()
+            return dot(rows_ref[...], stacked)
+
+        def precondition(k, solved, coarse_part, target):
+            pair_copy(k, part.at[k], part_in.at[k]).wait_recv()
+            combined = weigh(solved + dot(basis_ref[...], coarse_part + part_in[k]))
             target[...] = combined.reshape(faces, dofs, cases)
             return combined
 
+        def invert_block(j):
+            eliminate(inverse_ref, leaf_ref, panel_ref, entry_ref, j)
+
         def column_sum(value):
             return jnp.sum(value, axis=0, keepdims=True)
 
@@ -376,9 +399,33 @@
 
         halo_start(0, loads_ref)
         pair_copy(2, rows_ref, partner_rows).start()
+        own[1].wait()
+        own[2].wait()
+        scaling = 1.0 + masks_ref[...].astype(jnp.float32)
+        faces_in_leaf = LEAF // dofs
+        diagonal = lax.broadcasted_iota(jnp.int32, (LEAF, LEAF), 0) == lax.broadcasted_iota(
+            jnp.int32, (LEAF, LEAF), 1
+        )
+        blocks = [slice(i * LEAF, (i + 1) * LEAF) for i in range(order // LEAF)]
+        across = [
+            jnp.concatenate([scaling[i * faces_in_leaf + f : i * faces_in_leaf + f + 1] for f in range(faces_in_leaf)], axis=1)
+            for i in range(len(blocks))
+        ]
+        for i, rows in enumerate(blocks):
+            down = jnp.sum(jnp.where(diagonal, across[i], 0.0), axis=1, keepdims=True)
+            for j, columns in enumerate(blocks):
+                operator_ref[rows, columns] = down * operator_ref[rows, columns] * across[j]
+        inverse_ref[...] = operator_ref[...] + dot_right_transposed(basis_ref[...], basis_ref[...])
+        invert_block(0)
         halo_wait(0, loads_ref)
         r0 = flat(loads_ref) + flat(halo.at[0])
-        u0 = precondition(0, r0, unsummed.at[0])
+        weighted = weigh(r0)
+        gather_start(0, weighted)
+        invert_block(1)
+        pair_copy(2, rows_ref, partner_rows).wait_recv()
+        coarse_part = coarse_start(0)
+        invert_block(2)
+        u0 = precondition(0, dot(inverse_ref[...], weighted), coarse_part, unsummed.at[0])
         halo_start(1, unsummed.at[0])
         gamma_part = column_sum(r0 * u0)
         halo_wait(1, unsummed.at[0])
@@ -386,12 +433,15 @@
         t0 = dot(operator_ref[...], z0)
         unsummed[1] = t0.reshape(faces, dofs, cases)
         halo_start(2, unsummed.at[1])
-        pad = jnp.zeros((5, cases), jnp.float32)
-        sum_start(0, 0, jnp.concatenate([gamma_part, column_sum(z0 * t0), pad, pad[:1]], axis=0))
+        sum_start(0, 0, jnp.concatenate([gamma_part, column_sum(z0 * t0)], axis=0))
         halo_wait(2, unsummed.at[1])
         q0 = t0 + flat(halo.at[2])
+        weighted = weigh(q0)
+        gather_start(1, weighted)
+        solved = dot(inverse_ref[...], weighted)
         sum_start(0, 1, sum_end(0, 0))
-        u1 = precondition(1, q0, unsummed.at[2])
+        coarse_part = coarse_start(1)
+        u1 = precondition(1, solved, coarse_part, unsummed.at[2])
         halo_start(3, unsummed.at[2])
         sum_start(0, 2, sum_end(0, 1))
         halo_wait(3, unsummed.at[2])
@@ -409,7 +459,8 @@
             1,
             0,
             jnp.concatenate(
-                [column_sum(r1 * (u0 - step * u1)), column_sum(z1 * t1), column_sum(z0 * t1), pad], axis=0
+                [column_sum(r1 * (u0 - step * u1)), column_sum(z1 * t1), column_sum(z0 * t1), jnp.zeros_like(step)],
+                axis=0,
             ),
         )
         sum_start(1, 1, sum_end(1, 0))
@@ -430,14 +481,10 @@
         for k in range(2):
             gather_finish(k)
             pair_copy(k, part.at[k], part_in.at[k]).wait_send()
-            for buffer, send, recv, mine, count, device_of in stages:
-                spread_finish(buffer, send, recv, k, mine, count, device_of)
+            for buffers, send, recv, mine, count, device_of in stages:
+                spread_finish(buffers[k], send, recv, k, mine, count, device_of)
 
     return kernel
-
-
-def in_vmem(count):
-    return [pl.BlockSpec(memory_space=pltpu.VMEM)] * count
 
 
 def on_device(sizes, face_loads, schur_blocks, coarse_basis, drop_masks, coarse_inverse):
@@ -447,33 +494,41 @@
     faces, dofs, cases = face_loads.shape[2:]
     order = faces * dofs
     width = coarse_basis.shape[3]
-    square = jax.ShapeDtypeStruct((order, order), jnp.float32)
-    scaling = 1.0 + drop_masks.astype(jnp.float32)
-    operator, inverse = pl.pallas_call(
-        factor_kernel,
-        out_shape=[square, square],
-        in_specs=in_vmem(4),
-        out_specs=in_vmem(2),
-        scratch_shapes=[pltpu.VMEM((LEAF, LEAF), jnp.float32)],
-        compiler_params=pltpu.CompilerParams(vmem_limit_bytes=16 << 20),
-    )(schur_blocks[0, 0], coarse_basis[0, 0], scaling.reshape(order, 1), scaling.reshape(1, order))
     vector = jax.ShapeDtypeStruct((faces, dofs, cases), jnp.float32)
     dma = pltpu.SemaphoreType.DMA
     solved, residual = pl.pallas_call(
         make_iterate_kernel(sizes),
         out_shape=[vector, vector],
-        in_specs=in_vmem(5),
-        out_specs=in_vmem(2),
+        in_specs=[
+            pl.BlockSpec(memory_space=pl.ANY),
+            pl.BlockSpec(memory_space=pl.ANY),
+            pl.BlockSpec(memory_space=pl.ANY),
+            pl.BlockSpec(memory_space=pltpu.VMEM),
+            pl.BlockSpec(memory_space=pl.ANY),
+        ],
+        out_specs=[pl.BlockSpec(memory_space=pltpu.VMEM)] * 2,
         scratch_shapes=[
+            pltpu.VMEM((faces, dofs, cases), jnp.float32),
+            pltpu.VMEM((order, order), jnp.float32),
+            pltpu.VMEM((order, width), jnp.float32),
+            pltpu.VMEM((width, coarse_count * width), jnp.float32),
+            pltpu.VMEM((order, order), jnp.float32),
+            pltpu.VMEM((LEAF, LEAF), jnp.float32),
+            pltpu.VMEM((GROUP, LEAF), jnp.float32),
+            pltpu.VMEM((GROUP, GROUP, LEAF), jnp.float32),
             pltpu.VMEM((5, faces, dofs, cases), jnp.float32),
             pltpu.VMEM((4, faces, dofs, cases), jnp.float32),
             pltpu.VMEM((2, coarse_count, width, cases), jnp.float32),
             pltpu.VMEM((width, coarse_count * width), jnp.float32),
             pltpu.VMEM((2, width, cases), jnp.float32),
             pltpu.VMEM((2, width, cases), jnp.float32),
-            pltpu.VMEM((2, near_count, 8, cases), jnp.float32),
-            pltpu.VMEM((2, y_count, 8, cases), jnp.float32),
-            pltpu.VMEM((2, far_count, 8, cases), jnp.float32),
+            pltpu.VMEM((near_count, 2, cases), jnp.float32),
+            pltpu.VMEM((y_count, 2, cases), jnp.float32),
+            pltpu.VMEM((far_count, 2, cases), jnp.float32),
+            pltpu.VMEM((near_count, 4, cases), jnp.float32),
+            pltpu.VMEM((y_count, 4, cases), jnp.float32),
+            pltpu.VMEM((far_count, 4, cases), jnp.float32),
+            dma((4,)),
             dma((5, faces)),
             dma((5, faces)),
             dma((2, near_count)),
@@ -490,7 +545,7 @@
         compiler_params=pltpu.CompilerParams(
             collective_id=0, has_side_effects=True, vmem_limit_bytes=32 << 20
         ),
-    )(face_loads[0, 0], operator, inverse, coarse_basis[0, 0], coarse_inverse[0])
+    )(face_loads[0, 0], schur_blocks[0, 0], coarse_basis[0, 0], drop_masks[0, 0], coarse_inverse[0])
     return solved[None, None], residual[None, None]
 
 

time: 135 us -> 111 us (0.82)
  Pallas kernels: 130 us -> 106 us
    pallas_call x1 -> x0, Pallas kernels: 25.3 us -> none  [on_device(): pl.pallas_call(factor_kernel, out_shape=[square, square], in_specs=in_vme...]
    unnamed x13 -> x10, local copies, waits for them, and re-layouts: 3.85 us -> 4.1 us
where the time goes in v2:
time: 111 us; the launch traced here: 110 us
  Pallas kernels  106 us (95%)
  local copies, waits for them, and re-layouts  4.1 us (4%)
    pallas_call x1, Pallas kernels, on_device(): pl.pallas_call(make_iterate_kernel(sizes), out_shape=[vector, vector], in...  106 us
    unnamed x10, local copies, waits for them, and re-layouts  4.1 us

profile of v2, /device:TPU:1, one launch (start us, length us, event | category | flops | bytes accessed | tf_op | source)
XLA Modules:
  0.0 110.3 jit_solution(9743169206983380388)
XLA Ops:
  0.6 0.0 copy-start.1
  0.6 0.7 copy.10
  1.4 0.0 copy-start.2
  1.4 1.0 copy.7
  2.3 0.0 copy-done.1
  2.3 0.0 copy-done.2
  2.3 0.0 copy-start
  2.4 1.1 copy-done
  3.4 105.6 %shard_map.68 = (f32[6,64,128]{2,1,0:T(8,128)S(1)}, f32[6,64,128]{2,1,0:T(8,128)S(1)}) custom-call(f32[6,64,128]{2,1,0:T(8,128)S(1)} %bitcast.11, f32[384,384]{1,0:T(8,128)S(1)} %bitcast.10, f32[384,32]{1,0:T(8,128)S(1)} %bitcast.9, s32[6,64]{1,0:T(8,128)S(1)} %bitcast.15, f32[32,512]{1,0:T(8,128)S(1)} %bitcast.14), custom_call_target="tpu_custom_call" | custom-call | tf_op jit(solution)/shard_map/pallas_call | solution.py:499
  109.0 0.7 copy.13
  109.7 0.7 copy.14
Async XLA Ops:
  0.6 1.7 %copy-start.1 = (f32[1,1,6,64,128]{4,3,2,1,0:T(8,128)S(1)}, f32[1,1,6,64,128]{4,3,2,1,0:T(8,128)}, u32[]{:S(2)}) copy-start(f32[1,1,6,64,128]{4,3,2,1,0:T(8,128)} %param.5) | copy-start | bytes 589828
  1.4 1.0 copy-start.2
  2.3 1.1 copy-start

commit v3 on v2

--- a/solution.py
+++ b/solution.py
@@ -22,12 +22,6 @@
 def dot_left_transposed(former, latter):
     return lax.dot_general(
         former, latter, (((0,), (0,)), ((), ())), precision=highest, preferred_element_type=jnp.float32
-    )
-
-
-def dot_right_transposed(former, latter):
-    return lax.dot_general(
-        former, latter, (((1,), (1,)), ((), ())), precision=highest, preferred_element_type=jnp.float32
     )
 
 
@@ -55,18 +49,8 @@
         a, b, c = matrix[0][0], matrix[0][1], matrix[1][1]
         det = reciprocal(a * c - b * b)
         return [[c * det, -b * det], [-b * det, a * det]]
+    first, carried, second = halves(matrix)
     half = size // 2
-    corner = [row[half:] for row in matrix[:half]]
-    first = small_inverse([row[:half] for row in matrix[:half]])
-    carried = product(first, corner)
-    rest = [[None] * half for _ in range(half)]
-    for i in range(half):
-        for j in range(i, half):
-            total = matrix[half + i][half + j]
-            for t in range(half):
-                total = total - corner[t][i] * carried[t][j]
-            rest[i][j] = rest[j][i] = total
-    second = small_inverse(rest)
     side = product(carried, second)
     out = [[None] * size for _ in range(size)]
     for i in range(half):
@@ -81,6 +65,41 @@
     return out
 
 
+def halves(matrix):
+    half = len(matrix) // 2
+    corner = [row[half:] for row in matrix[:half]]
+    first = small_inverse([row[:half] for row in matrix[:half]])
+    carried = product(first, corner)
+    rest = [[None] * half for _ in range(half)]
+    for i in range(half):
+        for j in range(i, half):
+            total = matrix[half + i][half + j]
+            for t in range(half):
+                total = total - corner[t][i] * carried[t][j]
+            rest[i][j] = rest[j][i] = total
+    return first, carried, small_inverse(rest)
+
+
+def small_solve(matrix, right):
+    half = len(matrix) // 2
+    first, carried, second = halves(matrix)
+    lower = []
+    for i in range(half):
+        total = right[half + i]
+        for t in range(half):
+            total = total - carried[t][i] * right[t]
+        lower.append(total)
+    upper = [row[0] for row in product(first, [[value] for value in right[:half]])]
+    below = [row[0] for row in product(second, [[value] for value in lower])]
+    above = []
+    for i in range(half):
+        total = upper[i]
+        for t in range(half):
+            total = total - carried[i][t] * below[t]
+        above.append(total)
+    return above + below
+
+
 def invert_leaf(leaf_ref, panel_ref, entry_ref):
     shape = (GROUP, LEAF)
     lane = lax.broadcasted_iota(jnp.int32, shape, 1)
@@ -95,17 +114,10 @@
         for r in range(GROUP):
             for s in range(r, GROUP):
                 pivots[r][s] = pivots[s][r] = jnp.broadcast_to(entry_ref[s, r : r + 1, :], shape)
-        inverse = small_inverse(pivots)
         turned = jnp.where(lane >= last, 0.0, pltpu.roll(panel, last, 1))
         panel_ref[...] = jnp.where(lane == last + sublane, 1.0, turned)
         unit = [jnp.broadcast_to(panel_ref[t : t + 1, :], shape) for t in range(GROUP)]
-        solved = []
-        for s in range(GROUP):
-            total = inverse[s][0] * unit[0]
-            for t in range(1, GROUP):
-                total = total + inverse[s][t] * unit[t]
-            solved.append(total)
-        return solved
+        return small_solve(pivots, unit)
 
     def tile_of(solved):
         tile = solved[0]
@@ -164,14 +176,16 @@
     def kernel(
         loads_hbm, schur_hbm, basis_hbm, masks_ref, rows_hbm, solution_ref, residual_ref,
         loads_ref, operator_ref, basis_ref, rows_ref, inverse_ref, leaf_ref, panel_ref, entry_ref,
-        halo, unsummed, gathered, partner_rows, part, part_in, sums_1a, sums_1b, sums_1c, sums_2a, sums_2b, sums_2c,
-        own_sem,
+        halo, unsummed, gathered, partner_rows, part, part_in,
+        far_out, corner_out, corner_in, slice_out, slice_in, far_rows, own_out, own_in,
+        sums_1a, sums_1b, sums_1c, sums_2a, sums_2b, sums_2c,
+        own_sem, far_send, far_recv,
         halo_send, halo_recv, near_send, near_recv, pair_send, pair_recv,
         a_send, a_recv, b_send, b_recv, c_send, c_recv,
     ):
         faces, dofs, cases = loads_ref.shape
         order = faces * dofs
-        width = basis_ref.shape[1]
+        width = basis_ref.shape[0]
         coarse = lax.axis_index("coarse")
         sub = lax.axis_index("sub")
         core = coarse % core_count
@@ -248,36 +262,117 @@
         own[3].wait()
         pl.semaphore_wait(barrier, expected)
 
-        def halo_copy(k, source, face):
+        far_present = jnp.logical_or(
+            jnp.logical_and(core == 0, present[0]), jnp.logical_and(core == 1, present[1])
+        )
+        far_device_id = (coarse - 1 + 2 * core, sub)
+
+        @pl.when(jnp.logical_not(far_present))
+        def _():
+            for buffer in (corner_in, slice_in, far_rows, own_in):
+                buffer[...] = jnp.zeros_like(buffer)
+
+        def face_copy(k, source, face, device):
             return pltpu.make_async_remote_copy(
-                src_ref=source.at[face],
+                src_ref=source,
                 dst_ref=halo.at[k, face ^ 1],
                 send_sem=halo_send.at[k, face],
                 recv_sem=halo_recv.at[k, face ^ 1],
-                device_id=neighbour[face],
+                device_id=device,
                 device_id_type=MESH,
             )
 
-        def halo_start(k, source):
+        def near_faces(action):
             for face in range(faces):
-
-                @pl.when(present[face])
+                here = present[face]
+                if face < 2:
+                    here = jnp.logical_and(here, core != face)
+
+                @pl.when(here)
                 def _():
-                    halo_copy(k, source, face).start()
-
-        def halo_wait(k, source):
-            for face in range(faces):
-
-                @pl.when(present[face])
-                def _():
-                    halo_copy(k, source, face ^ 1).wait_recv()
-
-        def halo_finish(k, source):
-            for face in range(faces):
-
-                @pl.when(present[face])
-                def _():
-                    halo_copy(k, source, face).wait_send()
+                    action(face)
+
+        def near_start(k, source):
+            near_faces(lambda face: face_copy(k, source.at[face], face, neighbour[face]).start())
+
+        def near_wait(k):
+            near_faces(lambda face: face_copy(k, halo.at[k, face], face ^ 1, neighbour[face]).wait_recv())
+
+        def near_finish(k, source):
+            near_faces(lambda face: face_copy(k, source.at[face], face, neighbour[face]).wait_send())
+
+        def far_face_copy(k, source):
+            return pltpu.make_async_remote_copy(
+                src_ref=source,
+                dst_ref=halo.at[k, 1 - core],
+                send_sem=halo_send.at[k, core],
+                recv_sem=halo_recv.at[k, 1 - core],
+                device_id=far_device_id,
+                device_id_type=MESH,
+            )
+
+        def far_face_start(k, source):
+            @pl.when(far_present)
+            def _():
+                far_face_copy(k, source).start()
+
+        def far_face_wait(k):
+            @pl.when(far_present)
+            def _():
+                pltpu.make_async_remote_copy(
+                    src_ref=halo.at[k, core],
+                    dst_ref=halo.at[k, core],
+                    send_sem=halo_send.at[k, 1 - core],
+                    recv_sem=halo_recv.at[k, core],
+                    device_id=far_device_id,
+                    device_id_type=MESH,
+                ).wait_recv()
+
+        def far_face_finish(k, source):
+            @pl.when(far_present)
+            def _():
+                far_face_copy(k, source).wait_send()
+
+        def far_copy(n, source, target):
+            return pltpu.make_async_remote_copy(
+                src_ref=source,
+                dst_ref=target,
+                send_sem=far_send.at[n],
+                recv_sem=far_recv.at[n],
+                device_id=far_device_id,
+                device_id_type=MESH,
+            )
+
+        far_pairs = [(rows_ref, far_rows), (corner_out, corner_in), (slice_out, slice_in), (own_out, own_in)]
+
+        def far_start(n):
+            @pl.when(far_present)
+            def _():
+                far_copy(n, *far_pairs[n]).start()
+
+        def far_wait(n):
+            @pl.when(far_present)
+            def _():
+                far_copy(n, *far_pairs[n]).wait_recv()
+
+        def far_finish(n):
+            @pl.when(far_present)
+            def _():
+                far_copy(n, *far_pairs[n]).wait_send()
+
+        def near_incoming(k):
+            sibling = halo[k, 1 - core]
+            pieces = [jnp.where(core == 1, sibling, 0.0), jnp.where(core == 0, sibling, 0.0)]
+            return jnp.concatenate(pieces + [halo[k, face] for face in range(2, faces)], axis=0)
+
+        def on_far_face(value):
+            return jnp.concatenate([jnp.where(core == 0, value, 0.0), jnp.where(core == 1, value, 0.0)], axis=0)
+
+        def far_face_of(value):
+            return jnp.where(core == 0, value[:dofs], value[dofs : 2 * dofs])
+
+        def add_on_coarse_faces(value, extra):
+            return jnp.concatenate([value[: 2 * dofs] + extra, value[2 * dofs :]], axis=0)
 
         def pair_copy(k, source, target):
             return pltpu.make_async_remote_copy(
@@ -349,7 +444,7 @@
             return jnp.concatenate(pieces, axis=0)
 
         def gather_start(k, weighted):
-            gathered[k, coarse] = dot_left_transposed(basis_ref[...], weighted)
+            gathered[k, coarse] = dot(basis_ref[...], weighted)
 
             def body(j, carry):
                 index = (near + j) % near_count
@@ -384,7 +479,7 @@
 
         def precondition(k, solved, coarse_part, target):
             pair_copy(k, part.at[k], part_in.at[k]).wait_recv()
-            combined = weigh(solved + dot(basis_ref[...], coarse_part + part_in[k]))
+            combined = weigh(solved + dot_left_transposed(basis_ref[...], coarse_part + part_in[k]))
             target[...] = combined.reshape(faces, dofs, cases)
             return combined
 
@@ -397,7 +492,9 @@
         def flat(ref):
             return ref[...].reshape(order, cases)
 
-        halo_start(0, loads_ref)
+        near_start(0, loads_ref)
+        far_face_start(0, loads_ref.at[core])
+        far_start(0)
         pair_copy(2, rows_ref, partner_rows).start()
         own[1].wait()
         own[2].wait()
@@ -408,65 +505,98 @@
         )
         blocks = [slice(i * LEAF, (i + 1) * LEAF) for i in range(order // LEAF)]
         across = [
-            jnp.concatenate([scaling[i * faces_in_leaf + f : i * faces_in_leaf + f + 1] for f in range(faces_in_leaf)], axis=1)
+            jnp.concatenate([scaling[i * faces_in_leaf + f] for f in range(faces_in_leaf)], axis=1)
             for i in range(len(blocks))
         ]
         for i, rows in enumerate(blocks):
             down = jnp.sum(jnp.where(diagonal, across[i], 0.0), axis=1, keepdims=True)
             for j, columns in enumerate(blocks):
                 operator_ref[rows, columns] = down * operator_ref[rows, columns] * across[j]
-        inverse_ref[...] = operator_ref[...] + dot_right_transposed(basis_ref[...], basis_ref[...])
+        inverse_ref[...] = operator_ref[...] + dot_left_transposed(basis_ref[...], basis_ref[...])
+        half_of_lane = lax.broadcasted_iota(jnp.int32, (dofs, 2 * dofs), 1) // dofs
+        corner = jnp.where(core == 0, operator_ref[:dofs, : 2 * dofs], operator_ref[dofs : 2 * dofs, : 2 * dofs])
+        corner_out[...] = jnp.where(half_of_lane == core, corner, 0.0)
+        slice_out[...] = jnp.where(half_of_lane[:width] == core, basis_ref[:, : 2 * dofs], 0.0)
+        far_start(1)
+        far_start(2)
         invert_block(0)
-        halo_wait(0, loads_ref)
+        near_wait(0)
+        far_face_wait(0)
         r0 = flat(loads_ref) + flat(halo.at[0])
         weighted = weigh(r0)
         gather_start(0, weighted)
         invert_block(1)
         pair_copy(2, rows_ref, partner_rows).wait_recv()
+        for n in range(3):
+            far_wait(n)
         coarse_part = coarse_start(0)
         invert_block(2)
         u0 = precondition(0, dot(inverse_ref[...], weighted), coarse_part, unsummed.at[0])
-        halo_start(1, unsummed.at[0])
+        near_start(1, unsummed.at[0])
+        far_face_start(1, unsummed.at[0, core])
         gamma_part = column_sum(r0 * u0)
-        halo_wait(1, unsummed.at[0])
-        z0 = u0 + flat(halo.at[1])
-        t0 = dot(operator_ref[...], z0)
+        shared = unsummed[0, core]
+        near_wait(1)
+        near_z0 = u0 + near_incoming(1)
+        near_t0 = dot(operator_ref[...], near_z0)
+        far_out[0] = far_face_of(near_t0)
+        far_face_start(2, far_out.at[0])
+        corner_term = dot(corner_in[...], jnp.concatenate([shared, shared], axis=0))
+        far_face_wait(1)
+        arrived = on_far_face(halo[1, core])
+        z0 = add_on_coarse_faces(near_z0, arrived)
+        t0 = near_t0 + dot(operator_ref[:, : 2 * dofs], arrived)
         unsummed[1] = t0.reshape(faces, dofs, cases)
-        halo_start(2, unsummed.at[1])
+        near_start(2, unsummed.at[1])
         sum_start(0, 0, jnp.concatenate([gamma_part, column_sum(z0 * t0)], axis=0))
-        halo_wait(2, unsummed.at[1])
-        q0 = t0 + flat(halo.at[2])
+        near_wait(2)
+        near_q0 = t0 + near_incoming(2)
+        far_face_wait(2)
+        q0 = add_on_coarse_faces(near_q0, on_far_face(halo[2, core] + corner_term))
         weighted = weigh(q0)
         gather_start(1, weighted)
-        solved = dot(inverse_ref[...], weighted)
+        solved = weigh(dot(inverse_ref[...], weighted))
+        far_out[1] = far_face_of(solved)
+        far_face_start(3, far_out.at[1])
         sum_start(0, 1, sum_end(0, 0))
         coarse_part = coarse_start(1)
-        u1 = precondition(1, solved, coarse_part, unsummed.at[2])
-        halo_start(3, unsummed.at[2])
+        own_out[...] = coarse_part
+        far_start(3)
+        far_coarse = dot(far_rows[...], gathered[1].reshape(coarse_count * width, cases))
         sum_start(0, 2, sum_end(0, 1))
-        halo_wait(3, unsummed.at[2])
-        w0 = u1 + flat(halo.at[3])
+        pair_copy(1, part.at[1], part_in.at[1]).wait_recv()
+        u1 = solved + weigh(dot_left_transposed(basis_ref[...], coarse_part + part_in[1]))
+        unsummed[2] = u1.reshape(faces, dofs, cases)
+        near_start(3, unsummed.at[2])
+        far_wait(3)
+        far_face_wait(3)
+        spread = 0.5 * dot_left_transposed(slice_in[...], far_coarse + own_in[...])
+        far_w0 = add_on_coarse_faces(u1, on_far_face(halo[3, core] + spread[:dofs] + spread[dofs:]))
+        near_wait(3)
+        w0 = far_w0 + near_incoming(3)
         t1 = dot(operator_ref[...], w0)
         unsummed[3] = t1.reshape(faces, dofs, cases)
-        halo_start(4, unsummed.at[3])
+        near_start(4, unsummed.at[3])
+        far_face_start(4, unsummed.at[3, core])
         first = sum_end(0, 2)
         gamma, energy = first[0:1], first[1:2]
         step = gamma / energy
         z1 = z0 - step * w0
         r1 = r0 - step * q0
-        t1 = t0 - step * t1
+        t1_next = t0 - step * t1
         sum_start(
             1,
             0,
             jnp.concatenate(
-                [column_sum(r1 * (u0 - step * u1)), column_sum(z1 * t1), column_sum(z0 * t1), jnp.zeros_like(step)],
+                [column_sum(r1 * (u0 - step * u1)), column_sum(z1 * t1_next), column_sum(z0 * t1_next), jnp.zeros_like(step)],
                 axis=0,
             ),
         )
         sum_start(1, 1, sum_end(1, 0))
         sum_start(1, 2, sum_end(1, 1))
-        halo_wait(4, unsummed.at[3])
-        mapped = t1 + flat(halo.at[2]) - step * flat(halo.at[4])
+        near_wait(4)
+        far_face_wait(4)
+        mapped = q0 - step * (t1 + flat(halo.at[4]))
         second = sum_end(1, 2)
         gamma_next = second[0:1]
         ratio = gamma_next / gamma
@@ -474,9 +604,16 @@
         solution_ref[...] = (step * z0 + last * (z1 + ratio * z0)).reshape(faces, dofs, cases)
         residual_ref[...] = (r1 - last * (mapped + ratio * q0)).reshape(faces, dofs, cases)
 
-        halo_finish(0, loads_ref)
+        near_finish(0, loads_ref)
+        far_face_finish(0, loads_ref.at[core])
         for k in range(1, 5):
-            halo_finish(k, unsummed.at[k - 1])
+            near_finish(k, unsummed.at[k - 1])
+        far_face_finish(1, unsummed.at[0, core])
+        far_face_finish(2, far_out.at[0])
+        far_face_finish(3, far_out.at[1])
+        far_face_finish(4, unsummed.at[3, core])
+        for n in range(4):
+            far_finish(n)
         pair_copy(2, rows_ref, partner_rows).wait_send()
         for k in range(2):
             gather_finish(k)
@@ -510,7 +647,7 @@
         scratch_shapes=[
             pltpu.VMEM((faces, dofs, cases), jnp.float32),
             pltpu.VMEM((order, order), jnp.float32),
-            pltpu.VMEM((order, width), jnp.float32),
+            pltpu.VMEM((width, order), jnp.float32),
             pltpu.VMEM((width, coarse_count * width), jnp.float32),
             pltpu.VMEM((order, order), jnp.float32),
             pltpu.VMEM((LEAF, LEAF), jnp.float32),
@@ -522,12 +659,22 @@
             pltpu.VMEM((width, coarse_count * width), jnp.float32),
             pltpu.VMEM((2, width, cases), jnp.float32),
             pltpu.VMEM((2, width, cases), jnp.float32),
+            pltpu.VMEM((2, dofs, cases), jnp.float32),
+            pltpu.VMEM((dofs, 2 * dofs), jnp.float32),
+            pltpu.VMEM((dofs, 2 * dofs), jnp.float32),
+            pltpu.VMEM((width, 2 * dofs), jnp.float32),
+            pltpu.VMEM((width, 2 * dofs), jnp.float32),
+            pltpu.VMEM((width, coarse_count * width), jnp.float32),
+            pltpu.VMEM((width, cases), jnp.float32),
+            pltpu.VMEM((width, cases), jnp.float32),
             pltpu.VMEM((near_count, 2, cases), jnp.float32),
             pltpu.VMEM((y_count, 2, cases), jnp.float32),
             pltpu.VMEM((far_count, 2, cases), jnp.float32),
             pltpu.VMEM((near_count, 4, cases), jnp.float32),
             pltpu.VMEM((y_count, 4, cases), jnp.float32),
             pltpu.VMEM((far_count, 4, cases), jnp.float32),
+            dma((4,)),
+            dma((4,)),
             dma((4,)),
             dma((5, faces)),
             dma((5, faces)),
@@ -543,9 +690,9 @@
             dma((2, far_count)),
         ],
         compiler_params=pltpu.CompilerParams(
-            collective_id=0, has_side_effects=True, vmem_limit_bytes=32 << 20
+            collective_id=0, has_side_effects=True, vmem_limit_bytes=56 << 20
         ),
-    )(face_loads[0, 0], schur_blocks[0, 0], coarse_basis[0, 0], drop_masks[0, 0], coarse_inverse[0])
+    )(face_loads[0, 0], schur_blocks[0, 0], coarse_basis[0, 0].T, drop_masks[0].transpose(1, 0, 2), coarse_inverse[0])
     return solved[None, None], residual[None, None]
 
 

time: 111 us -> 112 us (level)
  Pallas kernels: 106 us -> 108 us
  local copies, waits for them, and re-layouts: 4.1 us -> 2.34 us
    pallas_call x1, Pallas kernels: 106 us -> 108 us  [on_device(): pl.pallas_call(make_iterate_kernel(sizes), out_shape=[vector, vector], in...]
    unnamed x10 -> x4, local copies, waits for them, and re-layouts: 4.1 us -> 2.34 us
where the time goes in v3:
time: 112 us; the launch traced here: 111 us
  Pallas kernels  108 us (96%)
  local copies, waits for them, and re-layouts  2.34 us (2%)
    pallas_call x1, Pallas kernels, on_device(): pl.pallas_call(make_iterate_kernel(sizes), out_shape=[vector, vector], in...  108 us
    unnamed x4, local copies, waits for them, and re-layouts  2.34 us

profile of v3, /device:TPU:1, one launch (start us, length us, event | category | flops | bytes accessed | tf_op | source)
XLA Modules:
  0.0 111.0 jit_solution(1649363485977255663)
XLA Ops:
  0.6 108.0 %shard_map.68 = (f32[6,64,128]{2,1,0:T(8,128)}, f32[6,64,128]{2,1,0:T(8,128)}) custom-call(f32[6,64,128]{2,1,0:T(8,128)} %bitcast.12, f32[384,384]{1,0:T(8,128)} %bitcast.9, f32[32,384]{1,0:T(8,128)} %bitcast.14, s32[6,1,64]{2,1,0:T(1,128)} %bitcast.15, f32[32,512]{1,0:T(8,128)} %bitcast.13), custom_call_target="tpu_custom_call" | custom-call | tf_op jit(solution)/shard_map/pallas_call | solution.py:636
  108.6 0.0 copy-start
  108.7 1.7 %copy.9 = f32[1,1,6,64,128]{4,3,2,1,0:T(8,128)} copy(f32[1,1,6,64,128]{4,3,2,1,0:T(8,128)} %bitcast.11) | data formatting | bytes 393216
  110.3 0.0 copy-done
  110.3 0.7 copy.10
Async XLA Ops:
  108.6 1.7 %copy-start = (f32[6,64,128]{2,1,0:T(8,128)S(1)}, f32[6,64,128]{2,1,0:T(8,128)}, u32[]{:S(2)}) copy-start(f32[6,64,128]{2,1,0:T(8,128)} %get-tuple-element.5) | copy-start | bytes 589828

commit v4 on v3

--- a/solution.py
+++ b/solution.py
@@ -10,6 +10,7 @@
 LOW_COUNT, Y_COUNT = 8, 8
 LEAF = 128
 GROUP = 8
+BEGIN_STEP, GATHER_STEP, COMBINE_STEP = 7, 7, 4
 
 MESH = pl.DeviceIdType.MESH
 highest = lax.Precision.HIGHEST
@@ -100,7 +101,7 @@
     return above + below
 
 
-def invert_leaf(leaf_ref, panel_ref, entry_ref):
+def invert_leaf(leaf_ref, panel_ref, entry_ref, visits):
     shape = (GROUP, LEAF)
     lane = lax.broadcasted_iota(jnp.int32, shape, 1)
     sublane = lax.broadcasted_iota(jnp.int32, shape, 0)
@@ -143,17 +144,23 @@
             leaf_ref[rows, :] = jnp.where(g == i, tile, jnp.where(g + 1 == i, panel, new[rows]))
         return following
 
-    solved = lax.fori_loop(0, LEAF // GROUP - 1, step, solve(leaf_ref[:GROUP, :]))
+    solved = solve(leaf_ref[:GROUP, :])
+    done = 0
+    for until, visit in list(visits) + [(LEAF // GROUP - 1, None)]:
+        solved = lax.fori_loop(done, until, step, solved)
+        done = until
+        if visit is not None:
+            visit()
     new = update(tile_of(solved))
     leaf_ref[:last, :] = new[:last]
     leaf_ref[last:, :] = tile_of(solved)
 
 
-def eliminate(matrix_ref, leaf_ref, panel_ref, entry_ref, j):
+def eliminate(matrix_ref, leaf_ref, panel_ref, entry_ref, j, visits=()):
     blocks = matrix_ref.shape[0] // LEAF
     here = slice(j * LEAF, (j + 1) * LEAF)
     leaf_ref[...] = matrix_ref[here, here]
-    invert_leaf(leaf_ref, panel_ref, entry_ref)
+    invert_leaf(leaf_ref, panel_ref, entry_ref, visits)
     inverse = leaf_ref[...]
     matrix_ref[here, here] = inverse
     others = [slice(i * LEAF, (i + 1) * LEAF) for i in range(blocks) if i != j]
@@ -174,15 +181,27 @@
     far_count = low_count * half_count
 
     def kernel(
-        loads_hbm, schur_hbm, basis_hbm, masks_ref, rows_hbm, solution_ref, residual_ref,
-        loads_ref, operator_ref, basis_ref, rows_ref, inverse_ref, leaf_ref, panel_ref, entry_ref,
-        halo, unsummed, gathered, partner_rows, part, part_in,
+        loads_hbm, schur_hbm, basis_hbm, masks_hbm, rows_hbm, solution_ref, residual_ref,
+        loads_ref, schur_ref, basis_ref, masks_ref, rows_ref, own_sem, start_ref, coarse_ref, operator_ref, inverse_ref, leaf_ref, panel_ref, entry_ref,
+        halo, unsummed, gathered, rows_own, rows_cross, partner_rows, part, part_in,
         far_out, corner_out, corner_in, slice_out, slice_in, far_rows, own_out, own_in,
         sums_1a, sums_1b, sums_1c, sums_2a, sums_2b, sums_2c,
-        own_sem, far_send, far_recv,
+        far_send, far_recv,
         halo_send, halo_recv, near_send, near_recv, pair_send, pair_recv,
         a_send, a_recv, b_send, b_recv, c_send, c_recv,
     ):
+        own = []
+        for n, (source, target) in enumerate(
+            [
+                (schur_hbm, schur_ref),
+                (basis_hbm, basis_ref),
+                (masks_hbm, masks_ref),
+                (loads_hbm, loads_ref),
+                (rows_hbm, rows_ref),
+            ]
+        ):
+            own.append(pltpu.make_async_copy(source, target, own_sem.at[n]))
+            own[n].start()
         faces, dofs, cases = loads_ref.shape
         order = faces * dofs
         width = basis_ref.shape[0]
@@ -223,21 +242,11 @@
             (coarse, sub + row_step),
         ]
 
-        own = []
-        for n, (source, target) in enumerate(
-            [(loads_hbm, loads_ref), (schur_hbm, operator_ref), (basis_hbm, basis_ref), (rows_hbm, rows_ref)]
-        ):
-            own.append(pltpu.make_async_copy(source, target, own_sem.at[n]))
-            own[n].start()
-
         barrier = pltpu.get_barrier_semaphore()
 
         def greet(device):
             pl.semaphore_signal(barrier, inc=1, device_id=device, device_id_type=MESH)
 
-        lax.fori_loop(1, near_count, lambda j, c: (greet(near_device((near + j) % near_count)), c)[1], 0)
-        lax.fori_loop(1, y_count, lambda j, c: (greet(y_device((y + j) % y_count)), c)[1], 0)
-        lax.fori_loop(1, far_count, lambda j, c: (greet(far_device((far + j) % far_count)), c)[1], 0)
         expected = near_count + y_count + far_count - 3
         for face in range(faces):
             expected = expected + present[face].astype(jnp.int32)
@@ -245,6 +254,10 @@
             @pl.when(present[face])
             def _():
                 greet(neighbour[face])
+
+        lax.fori_loop(1, far_count, lambda j, c: (greet(far_device((far + j) % far_count)), c)[1], 0)
+        lax.fori_loop(1, y_count, lambda j, c: (greet(y_device((y + j) % y_count)), c)[1], 0)
+        lax.fori_loop(1, near_count, lambda j, c: (greet(near_device((near + j) % near_count)), c)[1], 0)
 
         weights = [jnp.where(present[face], 0.5, 1.0) for face in range(faces)]
         for face in range(faces):
@@ -254,13 +267,6 @@
                 for k in range(halo.shape[0]):
                     halo[k, face] = jnp.zeros((dofs, cases), jnp.float32)
 
-        for k in range(gathered.shape[0]):
-            for index in range(near_count):
-                place = (index // core_count * half_count + (half_count - 1 - half)) * core_count + index % core_count
-                gathered[k, place] = jnp.zeros(gathered.shape[2:], jnp.float32)
-        own[0].wait()
-        own[3].wait()
-        pl.semaphore_wait(barrier, expected)
 
         far_present = jnp.logical_or(
             jnp.logical_and(core == 0, present[0]), jnp.logical_and(core == 1, present[1])
@@ -343,7 +349,7 @@
                 device_id_type=MESH,
             )
 
-        far_pairs = [(rows_ref, far_rows), (corner_out, corner_in), (slice_out, slice_in), (own_out, own_in)]
+        far_pairs = [(rows_cross, far_rows), (corner_out, corner_in), (slice_out, slice_in), (own_out, own_in)]
 
         def far_start(n):
             @pl.when(far_present)
@@ -444,38 +450,21 @@
             return jnp.concatenate(pieces, axis=0)
 
         def gather_start(k, weighted):
-            gathered[k, coarse] = dot(basis_ref[...], weighted)
-
-            def body(j, carry):
-                index = (near + j) % near_count
-                spread_copy(gathered.at[k], near_send, near_recv, k, coarse, near_device(index), coarse, index).start()
-                return carry
-
-            lax.fori_loop(1, near_count, body, 0)
+            gathered[k, near] = dot(basis_ref[...], weighted)
+            spread_start(gathered.at[k], near_send, near_recv, k, near, near_count, near_device)
 
         def gather_wait(k):
-            def body(j, carry):
-                index = (near + j) % near_count
-                device = near_device(index)
-                spread_copy(gathered.at[k], near_send, near_recv, k, coarse, device, device[0], index).wait_recv()
-                return carry
-
-            lax.fori_loop(1, near_count, body, 0)
+            spread_wait(gathered.at[k], near_send, near_recv, k, near, near_count, near_device)
 
         def gather_finish(k):
-            def body(j, carry):
-                index = (near + j) % near_count
-                spread_copy(gathered.at[k], near_send, near_recv, k, coarse, near_device(index), coarse, index).wait_send()
-                return carry
-
-            lax.fori_loop(1, near_count, body, 0)
+            spread_finish(gathered.at[k], near_send, near_recv, k, near, near_count, near_device)
 
         def coarse_start(k):
             gather_wait(k)
-            stacked = gathered[k].reshape(coarse_count * width, cases)
+            stacked = gathered[k].reshape(near_count * width, cases)
             part[k] = dot(partner_rows[...], stacked)
             pair_copy(k, part.at[k], part_in.at[k]).start()
-            return dot(rows_ref[...], stacked)
+            return dot(rows_own[...], stacked)
 
         def precondition(k, solved, coarse_part, target):
             pair_copy(k, part.at[k], part_in.at[k]).wait_recv()
@@ -483,8 +472,8 @@
             target[...] = combined.reshape(faces, dofs, cases)
             return combined
 
-        def invert_block(j):
-            eliminate(inverse_ref, leaf_ref, panel_ref, entry_ref, j)
+        def invert_block(j, *visits):
+            eliminate(inverse_ref, leaf_ref, panel_ref, entry_ref, j, visits)
 
         def column_sum(value):
             return jnp.sum(value, axis=0, keepdims=True)
@@ -492,12 +481,8 @@
         def flat(ref):
             return ref[...].reshape(order, cases)
 
-        near_start(0, loads_ref)
-        far_face_start(0, loads_ref.at[core])
-        far_start(0)
-        pair_copy(2, rows_ref, partner_rows).start()
-        own[1].wait()
-        own[2].wait()
+        for copy in own:
+            copy.wait()
         scaling = 1.0 + masks_ref[...].astype(jnp.float32)
         faces_in_leaf = LEAF // dofs
         diagonal = lax.broadcasted_iota(jnp.int32, (LEAF, LEAF), 0) == lax.broadcasted_iota(
@@ -511,27 +496,53 @@
         for i, rows in enumerate(blocks):
             down = jnp.sum(jnp.where(diagonal, across[i], 0.0), axis=1, keepdims=True)
             for j, columns in enumerate(blocks):
-                operator_ref[rows, columns] = down * operator_ref[rows, columns] * across[j]
+                operator_ref[rows, columns] = down * schur_ref[rows, columns] * across[j]
         inverse_ref[...] = operator_ref[...] + dot_left_transposed(basis_ref[...], basis_ref[...])
-        half_of_lane = lax.broadcasted_iota(jnp.int32, (dofs, 2 * dofs), 1) // dofs
-        corner = jnp.where(core == 0, operator_ref[:dofs, : 2 * dofs], operator_ref[dofs : 2 * dofs, : 2 * dofs])
-        corner_out[...] = jnp.where(half_of_lane == core, corner, 0.0)
-        slice_out[...] = jnp.where(half_of_lane[:width] == core, basis_ref[:, : 2 * dofs], 0.0)
-        far_start(1)
-        far_start(2)
-        invert_block(0)
-        near_wait(0)
-        far_face_wait(0)
-        r0 = flat(loads_ref) + flat(halo.at[0])
-        weighted = weigh(r0)
-        gather_start(0, weighted)
-        invert_block(1)
-        pair_copy(2, rows_ref, partner_rows).wait_recv()
-        for n in range(3):
-            far_wait(n)
-        coarse_part = coarse_start(0)
-        invert_block(2)
-        u0 = precondition(0, dot(inverse_ref[...], weighted), coarse_part, unsummed.at[0])
+
+        piece = core_count * width
+
+        def columns_of(which):
+            pieces = []
+            for index in range(x_count):
+                at = index * half_count * piece
+                pieces.append(
+                    jnp.where(which == 0, rows_ref[:, at : at + piece], rows_ref[:, at + piece : at + 2 * piece])
+                )
+            return jnp.concatenate(pieces, axis=1)
+
+        rows_cross[...] = columns_of(1 - half)
+        rows_own[...] = columns_of(half)
+        corner = jnp.where(core == 0, operator_ref[:dofs, :dofs], operator_ref[dofs : 2 * dofs, dofs : 2 * dofs])
+        corner_out[...] = jnp.concatenate([corner[: dofs // 2], corner[dofs // 2 :]], axis=1)
+        basis_slice = jnp.where(core == 0, basis_ref[:, :dofs], basis_ref[:, dofs : 2 * dofs])
+        slice_out[...] = jnp.concatenate([basis_slice[: width // 2], basis_slice[width // 2 :]], axis=1)
+
+        def begin():
+            pl.semaphore_wait(barrier, expected)
+            far_face_start(0, loads_ref.at[core])
+            near_start(0, loads_ref)
+
+        def send_rows():
+            pair_copy(2, rows_cross, partner_rows).start()
+
+        def gather_loads():
+            near_wait(0)
+            far_face_wait(0)
+            r0 = flat(loads_ref) + flat(halo.at[0])
+            start_ref[...] = r0
+            gather_start(0, weigh(r0))
+            for n in range(3):
+                far_start(n)
+
+        def combine_loads():
+            pair_copy(2, rows_cross, partner_rows).wait_recv()
+            coarse_ref[...] = coarse_start(0)
+
+        invert_block(0, (BEGIN_STEP, begin), (LEAF // GROUP - 1, send_rows))
+        invert_block(1, (GATHER_STEP, gather_loads))
+        invert_block(2, (COMBINE_STEP, combine_loads))
+        r0 = start_ref[...]
+        u0 = precondition(0, dot(inverse_ref[...], weigh(r0)), coarse_ref[...], unsummed.at[0])
         near_start(1, unsummed.at[0])
         far_face_start(1, unsummed.at[0, core])
         gamma_part = column_sum(r0 * u0)
@@ -541,7 +552,10 @@
         near_t0 = dot(operator_ref[...], near_z0)
         far_out[0] = far_face_of(near_t0)
         far_face_start(2, far_out.at[0])
-        corner_term = dot(corner_in[...], jnp.concatenate([shared, shared], axis=0))
+        for n in range(3):
+            far_wait(n)
+        corner = jnp.concatenate([corner_in[:, :dofs], corner_in[:, dofs:]], axis=0)
+        corner_term = dot(corner, shared)
         far_face_wait(1)
         arrived = on_far_face(halo[1, core])
         z0 = add_on_coarse_faces(near_z0, arrived)
@@ -562,7 +576,7 @@
         coarse_part = coarse_start(1)
         own_out[...] = coarse_part
         far_start(3)
-        far_coarse = dot(far_rows[...], gathered[1].reshape(coarse_count * width, cases))
+        far_coarse = dot(far_rows[...], gathered[1].reshape(near_count * width, cases))
         sum_start(0, 2, sum_end(0, 1))
         pair_copy(1, part.at[1], part_in.at[1]).wait_recv()
         u1 = solved + weigh(dot_left_transposed(basis_ref[...], coarse_part + part_in[1]))
@@ -570,8 +584,9 @@
         near_start(3, unsummed.at[2])
         far_wait(3)
         far_face_wait(3)
-        spread = 0.5 * dot_left_transposed(slice_in[...], far_coarse + own_in[...])
-        far_w0 = add_on_coarse_faces(u1, on_far_face(halo[3, core] + spread[:dofs] + spread[dofs:]))
+        basis_slice = jnp.concatenate([slice_in[:, :dofs], slice_in[:, dofs:]], axis=0)
+        spread = 0.5 * dot_left_transposed(basis_slice, far_coarse + own_in[...])
+        far_w0 = add_on_coarse_faces(u1, on_far_face(halo[3, core] + spread))
         near_wait(3)
         w0 = far_w0 + near_incoming(3)
         t1 = dot(operator_ref[...], w0)
@@ -614,7 +629,7 @@
         far_face_finish(4, unsummed.at[3, core])
         for n in range(4):
             far_finish(n)
-        pair_copy(2, rows_ref, partner_rows).wait_send()
+        pair_copy(2, rows_cross, partner_rows).wait_send()
         for k in range(2):
             gather_finish(k)
             pair_copy(k, part.at[k], part_in.at[k]).wait_send()
@@ -636,35 +651,36 @@
     solved, residual = pl.pallas_call(
         make_iterate_kernel(sizes),
         out_shape=[vector, vector],
-        in_specs=[
-            pl.BlockSpec(memory_space=pl.ANY),
-            pl.BlockSpec(memory_space=pl.ANY),
-            pl.BlockSpec(memory_space=pl.ANY),
-            pl.BlockSpec(memory_space=pltpu.VMEM),
-            pl.BlockSpec(memory_space=pl.ANY),
-        ],
+        in_specs=[pl.BlockSpec(memory_space=pl.ANY)] * 5,
         out_specs=[pl.BlockSpec(memory_space=pltpu.VMEM)] * 2,
         scratch_shapes=[
             pltpu.VMEM((faces, dofs, cases), jnp.float32),
             pltpu.VMEM((order, order), jnp.float32),
             pltpu.VMEM((width, order), jnp.float32),
+            pltpu.VMEM((faces, 1, dofs), jnp.int32),
             pltpu.VMEM((width, coarse_count * width), jnp.float32),
+            dma((5,)),
+            pltpu.VMEM((order, cases), jnp.float32),
+            pltpu.VMEM((width, cases), jnp.float32),
+            pltpu.VMEM((order, order), jnp.float32),
             pltpu.VMEM((order, order), jnp.float32),
             pltpu.VMEM((LEAF, LEAF), jnp.float32),
             pltpu.VMEM((GROUP, LEAF), jnp.float32),
             pltpu.VMEM((GROUP, GROUP, LEAF), jnp.float32),
             pltpu.VMEM((5, faces, dofs, cases), jnp.float32),
             pltpu.VMEM((4, faces, dofs, cases), jnp.float32),
-            pltpu.VMEM((2, coarse_count, width, cases), jnp.float32),
-            pltpu.VMEM((width, coarse_count * width), jnp.float32),
+            pltpu.VMEM((2, near_count, width, cases), jnp.float32),
+            pltpu.VMEM((width, near_count * width), jnp.float32),
+            pltpu.VMEM((width, near_count * width), jnp.float32),
+            pltpu.VMEM((width, near_count * width), jnp.float32),
             pltpu.VMEM((2, width, cases), jnp.float32),
             pltpu.VMEM((2, width, cases), jnp.float32),
             pltpu.VMEM((2, dofs, cases), jnp.float32),
-            pltpu.VMEM((dofs, 2 * dofs), jnp.float32),
-            pltpu.VMEM((dofs, 2 * dofs), jnp.float32),
-            pltpu.VMEM((width, 2 * dofs), jnp.float32),
-            pltpu.VMEM((width, 2 * dofs), jnp.float32),
-            pltpu.VMEM((width, coarse_count * width), jnp.float32),
+            pltpu.VMEM((dofs // 2, 2 * dofs), jnp.float32),
+            pltpu.VMEM((dofs // 2, 2 * dofs), jnp.float32),
+            pltpu.VMEM((width // 2, 2 * dofs), jnp.float32),
+            pltpu.VMEM((width // 2, 2 * dofs), jnp.float32),
+            pltpu.VMEM((width, near_count * width), jnp.float32),
             pltpu.VMEM((width, cases), jnp.float32),
             pltpu.VMEM((width, cases), jnp.float32),
             pltpu.VMEM((near_count, 2, cases), jnp.float32),
@@ -675,11 +691,10 @@
             pltpu.VMEM((far_count, 4, cases), jnp.float32),
             dma((4,)),
             dma((4,)),
-            dma((4,)),
             dma((5, faces)),
             dma((5, faces)),
             dma((2, near_count)),
-            dma((2, coarse_count)),
+            dma((2, near_count)),
             dma((3,)),
             dma((3,)),
             dma((2, near_count)),

time: 112 us -> 101 us (0.902)
  Pallas kernels: 108 us -> 98.1 us
    pallas_call x1, Pallas kernels: 108 us -> 98.1 us  [on_device(): pl.pallas_call(make_iterate_kernel(sizes), out_shape=[vector, vector], in...]
where the time goes in v4:
time: 101 us
  Pallas kernels  98.1 us (97%)
  local copies, waits for them, and re-layouts  2.34 us (2%)
    pallas_call x1, Pallas kernels, on_device(): pl.pallas_call(make_iterate_kernel(sizes), out_shape=[vector, vector], in...  98.1 us
    unnamed x4, local copies, waits for them, and re-layouts  2.34 us

profile of v4, /device:TPU:1, one launch (start us, length us, event | category | flops | bytes accessed | tf_op | source)
XLA Modules:
  0.0 101.0 jit_solution(12316214619235847292)
XLA Ops:
  0.6 98.1 %shard_map.68 = (f32[6,64,128]{2,1,0:T(8,128)}, f32[6,64,128]{2,1,0:T(8,128)}) custom-call(f32[6,64,128]{2,1,0:T(8,128)} %bitcast.12, f32[384,384]{1,0:T(8,128)} %bitcast.9, f32[32,384]{1,0:T(8,128)} %bitcast.14, s32[6,1,64]{2,1,0:T(1,128)} %bitcast.15, f32[32,512]{1,0:T(8,128)} %bitcast.13), custom_call_target="tpu_custom_call" | custom-call | tf_op jit(solution)/shard_map/pallas_call | solution.py:651
  98.7 0.0 copy-start
  98.7 1.7 %copy.9 = f32[1,1,6,64,128]{4,3,2,1,0:T(8,128)} copy(f32[1,1,6,64,128]{4,3,2,1,0:T(8,128)} %bitcast.11) | data formatting | bytes 393216
  100.4 0.0 copy-done
  100.4 0.7 copy.10
Async XLA Ops:
  98.7 1.7 %copy-start = (f32[6,64,128]{2,1,0:T(8,128)S(1)}, f32[6,64,128]{2,1,0:T(8,128)}, u32[]{:S(2)}) copy-start(f32[6,64,128]{2,1,0:T(8,128)} %get-tuple-element.5) | copy-start | bytes 589828
